TPU v7x, 32 devices: a whole 2x2x4 slice. The times are simulated.
32 devices in a mesh: parts: 2 (over x), tile: 16 (over z, y, core).
Axes of the slice: x: 2, y: 2, z: 4, core: 2. Of those that a mesh axis runs over, the one named last changes fastest.
Arguments:
- tiles: bfloat16 [64, 16, 16, 256], P(('parts', 'tile')), parts along dimension 0, may hold values from -6 to 6
- source_device: int32 [64, 8, 1], P(('parts', 'tile')), parts along dimension 0, may hold values from 0 to 15; in each aligned block of 16 rows (0 to 15, 16 to 31, ..., all dimensions but the last counted through in order) at most 2 rows name the same one
- source_slot: int32 [64, 8], P(('parts', 'tile')), parts along dimension 0, may hold values from 0 to 1
- present: int32 [64, 8], P(('parts', 'tile')), parts along dimension 0, may hold values 0 or 1
- depth_kernel: float32 [2, 49, 256], replicated, may hold values from -10 to 10
- norm_gain: float32 [2, 256], replicated, may hold values from 0.1 to 1.9
- w_in: bfloat16 [2, 256, 1024], replicated, may hold values from -0.375 to 0.375
- w_out: bfloat16 [2, 1024, 256], replicated, may hold values from -0.1875 to 0.1875
- cotangent: bfloat16 [64, 16, 16, 256], P(('parts', 'tile')), parts along dimension 0, may hold values from -6 to 6
Outputs:
- grad_tiles: bfloat16 [64, 16, 16, 256], P(('parts', 'tile')), parts along dimension 0
- grad_in: float32 [512, 2, 1024], P(('parts', 'tile')), parts along dimension 0
- grad_out: float32 [512, 2, 1024], P(('parts', 'tile')), parts along dimension 0
- grad_kernel: float32 [4, 49, 256], P('parts'), parts along dimension 0
- grad_gain: float32 [4, 256], P('parts'), parts along dimension 0
There are 2 independent parts, one for each index of `parts`. A program takes and returns all parts, laid end to end along the dimension named above; an argument that names none is the same for every part. Nothing has to cross between parts.
Inputs may be any that keep to these rules, and one draw needn't show every extreme that they name: `source_device`: among the 16 rows of one device (its tiles times the 8 directions) no device index appears more than 2 times, and 2 is reached.
All inputs are finite; a program needn't handle non-finite values. No bound on the sum of `present` on one device may be relied on, other than what follows from the above.
Results may differ from a plain program's by a relative error of at most 0.007.
Values may be sent and summed in bfloat16 or wider, within the bound.
A program may use at most 128 MiB of HBM per device.

v0:
```python
import math

import jax
import jax.numpy as jnp
from jax import lax
from jax.experimental import pallas as pl
from jax.experimental.pallas import tpu as pltpu
from jax.sharding import PartitionSpec as P

STRIP_KINDS = (1, 0, 3, 2, 1, 1, 0, 0)
NORM_EPSILON = 1e-06
ROOT_HALF = 0.7071067811865476
INV_ROOT_TWO_PI = 0.3989422804014327


def gelu_value(values):
    return values * 0.5 * (1.0 + lax.erf(values * ROOT_HALF))


def gelu_slope(values):
    return 0.5 * (1.0 + lax.erf(values * ROOT_HALF)) + values * INV_ROOT_TWO_PI * jnp.exp(
        -0.5 * values * values
    )


LANES = 128
SMEM = pl.BlockSpec(memory_space=pltpu.SMEM)
VMEM = pl.BlockSpec(memory_space=pltpu.VMEM)


def serve_kernel(wanted_ref, inputs_ref, out_ref, wide_ref, table_ref):
    for tile in range(inputs_ref.shape[0]):
        wide_ref[...] = inputs_ref[tile].astype(jnp.float32)
        table_ref[4 * tile] = wide_ref[0:3]
        table_ref[4 * tile + 1] = wide_ref[13:16]
        for depth in range(3):
            for place in range(16):
                row = pl.ds(place, 1)
                table_ref[4 * tile + 2, depth, row] = wide_ref[place, pl.ds(depth, 1)]
                table_ref[4 * tile + 3, depth, row] = wide_ref[place, pl.ds(13 + depth, 1)]

    def one(slot, carry):
        code = wanted_ref[slot]
        strip = table_ref[jnp.maximum(code, 0)]
        out_ref[slot] = jnp.where(code >= 0, strip, 0.0).astype(out_ref.dtype)
        return carry

    lax.fori_loop(0, out_ref.shape[0], one, 0)


def serve(inputs, wanted):
    tiles, extent, _, channels = inputs.shape
    return pl.pallas_call(
        serve_kernel,
        out_shape=jax.ShapeDtypeStruct((wanted.shape[0], 3, extent, channels), jnp.bfloat16),
        in_specs=[SMEM, VMEM],
        out_specs=VMEM,
        scratch_shapes=[
            pltpu.VMEM((extent, extent, channels), jnp.float32),
            pltpu.VMEM((4 * tiles, 3, extent, channels), jnp.float32),
        ],
        compiler_params=pltpu.CompilerParams(vmem_limit_bytes=32 * 1024 * 1024),
        name="serve",
    )(wanted, inputs)


def shift_columns(padded_ref, tile, shifted_ref):
    for tap_col in range(7):
        shifted_ref[tap_col] = padded_ref[tile, :, tap_col : tap_col + 16, :]


def forward_kernel(
    slot_ref, present_ref, inputs_ref, incoming_ref, kernel_ref, padded_ref, conv_ref, piece_ref, shifted_ref
):
    for tile in range(inputs_ref.shape[0]):

        def piece(direction):
            row = 8 * tile + direction
            strip = incoming_ref[slot_ref[row]].astype(jnp.float32)
            return jnp.where(present_ref[row] > 0, strip, 0.0)

        padded_ref[tile, 3:19, 3:19, :] = inputs_ref[tile].astype(jnp.float32)
        padded_ref[tile, 0:3, 3:19, :] = piece(0)
        padded_ref[tile, 19:22, 3:19, :] = piece(1)
        for direction, first in ((2, 0), (3, 19)):
            piece_ref[...] = piece(direction)
            for depth in range(3):
                for place in range(16):
                    padded_ref[tile, 3 + place, pl.ds(first + depth, 1)] = piece_ref[
                        depth, pl.ds(place, 1)
                    ]
        for direction, top, left, taken in ((4, 0, 0, 13), (5, 0, 19, 0), (6, 19, 0, 13), (7, 19, 19, 0)):
            piece_ref[...] = piece(direction)
            padded_ref[tile, top : top + 3, left : left + 3, :] = piece_ref[:, taken : taken + 3, :]
        padded_ref[tile, :, 22:24, :] = jnp.zeros((22, 2, padded_ref.shape[3]), jnp.float32)
        shift_columns(padded_ref, tile, shifted_ref)
        for half in range(conv_ref.shape[3] // LANES):
            lanes = pl.ds(half * LANES, LANES)

            def rows(step, carry):
                top = step * 4
                sums = [jnp.zeros((16, LANES), jnp.float32)] * 4
                for tap_col in range(7):
                    window = [shifted_ref[tap_col, top + row, :, lanes] for row in range(10)]
                    for tap_row in range(7):
                        weight = kernel_ref[pl.ds(7 * tap_row + tap_col, 1), lanes]
                        sums = [sums[row] + window[row + tap_row] * weight for row in range(4)]
                for row in range(4):
                    conv_ref[tile, top + row, :, lanes] = sums[row]
                return carry

            lax.fori_loop(0, 4, rows, 0)


def forward_conv(inputs, incoming, slot_index, present, kernel):
    tiles, extent, _, channels = inputs.shape
    return pl.pallas_call(
        forward_kernel,
        out_shape=(
            jax.ShapeDtypeStruct((tiles, extent + 6, extent + 8, channels), jnp.float32),
            jax.ShapeDtypeStruct((tiles, extent, extent, channels), jnp.float32),
        ),
        in_specs=[SMEM, SMEM, VMEM, VMEM, VMEM],
        out_specs=(VMEM, VMEM),
        scratch_shapes=[
            pltpu.VMEM((3, extent, channels), jnp.float32),
            pltpu.VMEM((7, extent + 6, extent, channels), jnp.float32),
        ],
        compiler_params=pltpu.CompilerParams(vmem_limit_bytes=32 * 1024 * 1024),
        name="forward_conv",
    )(slot_index, present, inputs, incoming, kernel)


def backward_kernel(
    slot_ref, present_ref, padded_ref, slopes_ref, kernel_ref,
    centre_ref, outgoing_ref, taps_ref, piece_ref, shifted_ref, border_ref, sums_ref, back_ref,
):
    channels = slopes_ref.shape[3]
    outgoing_ref[...] = jnp.zeros(outgoing_ref.shape, outgoing_ref.dtype)
    border_ref[...] = jnp.zeros(border_ref.shape, jnp.float32)
    for tile in range(slopes_ref.shape[0]):
        shift_columns(padded_ref, tile, shifted_ref)
        for tap_col in range(7):
            border_ref[tap_col, 6:22, tap_col : tap_col + 16, :] = slopes_ref[tile]
        for half in range(channels // LANES):
            lanes = pl.ds(half * LANES, LANES)

            def taps(tap_col, carry):
                def rows(step, sums):
                    top = step * 4
                    slopes = [slopes_ref[tile, top + row, :, lanes] for row in range(4)]
                    window = [shifted_ref[tap_col, top + row, :, lanes] for row in range(10)]
                    return tuple(
                        sums[tap_row]
                        + (
                            window[tap_row] * slopes[0]
                            + window[tap_row + 1] * slopes[1]
                            + window[tap_row + 2] * slopes[2]
                            + window[tap_row + 3] * slopes[3]
                        )
                        for tap_row in range(7)
                    )

                sums = lax.fori_loop(0, 4, rows, (jnp.zeros((16, LANES), jnp.float32),) * 7)
                for tap_row in range(7):
                    if tile == 0:
                        sums_ref[tap_col, tap_row, :, lanes] = sums[tap_row]
                    else:
                        sums_ref[tap_col, tap_row, :, lanes] += sums[tap_row]
                return carry

            lax.fori_loop(0, 7, taps, 0)

            def rows_back(step, carry):
                top = step * 2
                sums = [jnp.zeros((24, LANES), jnp.float32)] * 2
                for tap_col in range(7):
                    window = [border_ref[tap_col, top + row, :, lanes] for row in range(8)]
                    for tap_row in range(7):
                        weight = kernel_ref[pl.ds(7 * tap_row + tap_col, 1), lanes]
                        sums = [sums[row] + window[row + 6 - tap_row] * weight for row in range(2)]
                for row in range(2):
                    back_ref[top + row, :, lanes] = sums[row]
                return carry

            lax.fori_loop(0, 11, rows_back, 0)

        centre_ref[tile] = back_ref[3:19, 3:19, :]

        def send(direction):
            row = 8 * tile + direction
            strip = jnp.where(present_ref[row] > 0, piece_ref[...], 0.0)
            outgoing_ref[slot_ref[row]] = strip.astype(outgoing_ref.dtype)

        piece_ref[...] = back_ref[0:3, 3:19, :]
        send(0)
        piece_ref[...] = back_ref[19:22, 3:19, :]
        send(1)
        for direction, first in ((2, 0), (3, 19)):
            for depth in range(3):
                for place in range(16):
                    piece_ref[depth, pl.ds(place, 1)] = back_ref[
                        3 + place, pl.ds(first + depth, 1)
                    ]
            send(direction)
        for direction, top, left, taken in ((4, 0, 0, 13), (5, 0, 19, 0), (6, 19, 0, 13), (7, 19, 19, 0)):
            piece_ref[...] = jnp.zeros(piece_ref.shape, jnp.float32)
            piece_ref[:, taken : taken + 3, :] = back_ref[top : top + 3, left : left + 3, :]
            send(direction)
    for tap_col in range(7):
        for tap_row in range(7):
            taps_ref[pl.ds(7 * tap_row + tap_col, 1)] = jnp.sum(
                sums_ref[tap_col, tap_row], axis=0, keepdims=True
            )


def backward_conv(padded, back_conv, slot_index, present, kernel, slots):
    tiles, extent, _, channels = back_conv.shape
    return pl.pallas_call(
        backward_kernel,
        out_shape=(
            jax.ShapeDtypeStruct(back_conv.shape, jnp.float32),
            jax.ShapeDtypeStruct((slots, 3, extent, channels), jnp.bfloat16),
            jax.ShapeDtypeStruct((49, channels), jnp.float32),
        ),
        in_specs=[SMEM, SMEM, VMEM, VMEM, VMEM],
        out_specs=(VMEM, VMEM, VMEM),
        scratch_shapes=[
            pltpu.VMEM((3, extent, channels), jnp.float32),
            pltpu.VMEM((7, extent + 6, extent, channels), jnp.float32),
            pltpu.VMEM((7, extent + 12, extent + 8, channels), jnp.float32),
            pltpu.VMEM((7, 7, extent, channels), jnp.float32),
            pltpu.VMEM((extent + 6, extent + 8, channels), jnp.float32),
        ],
        compiler_params=pltpu.CompilerParams(vmem_limit_bytes=48 * 1024 * 1024),
        name="backward_conv",
    )(slot_index, present, padded, back_conv, kernel)


def collect_kernel(wanted_ref, base_ref, centre_ref, returned_ref, out_ref, table_ref):
    table_ref[...] = jnp.zeros(table_ref.shape, jnp.float32)

    def one(slot, carry):
        code = wanted_ref[slot]
        strip = returned_ref[slot].astype(jnp.float32)
        table_ref[jnp.maximum(code, 0)] += jnp.where(code >= 0, strip, 0.0)
        return carry

    lax.fori_loop(0, returned_ref.shape[0], one, 0)
    for tile in range(base_ref.shape[0]):
        out_ref[tile] = base_ref[tile].astype(jnp.float32) + centre_ref[tile]
        out_ref[tile, 0:3] += table_ref[4 * tile]
        out_ref[tile, 13:16] += table_ref[4 * tile + 1]
        for depth in range(3):
            for place in range(16):
                row = pl.ds(place, 1)
                out_ref[tile, place, pl.ds(depth, 1)] += table_ref[4 * tile + 2, depth, row]
                out_ref[tile, place, pl.ds(13 + depth, 1)] += table_ref[4 * tile + 3, depth, row]


def collect(base, centre, returned, wanted):
    tiles, extent, _, channels = base.shape
    return pl.pallas_call(
        collect_kernel,
        out_shape=jax.ShapeDtypeStruct(base.shape, jnp.float32),
        in_specs=[SMEM, VMEM, VMEM, VMEM],
        out_specs=VMEM,
        scratch_shapes=[pltpu.VMEM((4 * tiles, 3, extent, channels), jnp.float32)],
        compiler_params=pltpu.CompilerParams(vmem_limit_bytes=32 * 1024 * 1024),
        name="collect",
    )(wanted, base, centre, returned)


def normalize(conv, gain):
    average = jnp.mean(conv, axis=-1, keepdims=True)
    centred = conv - average
    spread = jnp.mean(centred * centred, axis=-1, keepdims=True)
    inverse = lax.rsqrt(spread + NORM_EPSILON)
    unit = centred * inverse
    return (unit, inverse, (unit * gain).astype(jnp.bfloat16))


def build_routes(source_device, source_slot, peers, capacity):
    row_total = source_slot.shape[0] * source_slot.shape[1]
    owner = source_device.reshape(row_total)
    codes = (source_slot * 4 + jnp.asarray(STRIP_KINDS, jnp.int32)[None, :]).reshape(row_total)
    later_rows = lax.broadcasted_iota(jnp.int32, (row_total, row_total), 0)
    other_rows = lax.broadcasted_iota(jnp.int32, (row_total, row_total), 1)
    before = jnp.logical_and(owner[:, None] == owner[None, :], other_rows < later_rows)
    ranking = jnp.sum(before.astype(jnp.int32), axis=1)
    slot_index = owner * capacity + ranking
    places = lax.broadcasted_iota(jnp.int32, (peers * capacity, row_total), 0)
    matched = (places == slot_index[None, :]).astype(jnp.int32)
    request = jnp.sum(matched * (codes[None, :] + 1), axis=1) - 1
    return (slot_index, request.reshape(peers, capacity))


def pair_term(operand_set):
    row_block, slope, rounded, hidden = operand_set
    dims_rows = (((0,), (0,)), ((), ()))
    first_term = lax.dot_general(row_block, slope, dims_rows, preferred_element_type=jnp.float32)
    second_term = lax.dot_general(rounded, hidden, dims_rows, preferred_element_type=jnp.float32)
    return jnp.stack([first_term, second_term], axis=1)


def halve(values, steps):
    index = lax.axis_index("tile")
    peers = 1 << steps
    values = values.reshape((peers, -1) + values.shape[1:])
    for step in range(steps):
        pairs = values.reshape((-1, 2) + values.shape[1:])
        bit = (index >> step) & 1
        kept = jnp.where(bit == 1, pairs[:, 1], pairs[:, 0])
        sent = jnp.where(bit == 1, pairs[:, 0], pairs[:, 1]).astype(jnp.bfloat16)
        partners = [(place, place ^ (1 << step)) for place in range(peers)]
        values = kept + lax.ppermute(sent, "tile", partners).astype(jnp.float32)
    return values[0]


def double(values, steps):
    peers = 1 << steps
    for step in range(steps):
        partners = [(place, place ^ (1 << step)) for place in range(peers)]
        values = values + lax.ppermute(values, "tile", partners)
    return values


def exchange(blocks, peers):
    arranged = blocks.reshape((peers, -1) + blocks.shape[1:])
    returned = lax.all_to_all(arranged, "tile", split_axis=0, concat_axis=0, tiled=True)
    return returned.reshape(blocks.shape)


def body(
    tiles, source_device, source_slot, present, depth_kernel, norm_gain, w_in, w_out, cotangent
):
    peers = lax.axis_size("tile")
    local_tiles = tiles.shape[0]
    extent = tiles.shape[1]
    channels = tiles.shape[3]
    layers = w_in.shape[0]
    capacity = max(2, 2 * ((8 * local_tiles + peers - 1) // peers))
    scale = 1.0 / math.sqrt(local_tiles * peers * extent * extent)
    slot_index, request = build_routes(source_device, source_slot, peers, capacity)
    wanted = lax.all_to_all(request, "tile", split_axis=0, concat_axis=0, tiled=True).reshape(-1)
    present = present.reshape(-1)
    dims_cols = (((1,), (1,)), ((), ()))
    saved = []
    current = tiles
    for layer_index in range(layers):
        incoming = exchange(serve(current, wanted), peers)
        padded, conv = forward_conv(
            current, incoming, slot_index, present, depth_kernel[layer_index]
        )
        unit, inverse, normed = normalize(conv, norm_gain[layer_index])
        row_block = normed.reshape(-1, channels)
        pre = jnp.dot(row_block, w_in[layer_index], preferred_element_type=jnp.float32)
        hidden = gelu_value(pre).astype(jnp.bfloat16)
        mixed = jnp.dot(hidden, w_out[layer_index], preferred_element_type=jnp.float32)
        kept = padded
        saved.append(
            (
                current,
                kept,
                unit.reshape(-1, channels),
                inverse.reshape(-1, 1),
                row_block,
                pre,
                hidden,
            )
        )
        current = (current.astype(jnp.float32) + mixed.reshape(current.shape)).astype(jnp.bfloat16)
    gradient = cotangent.astype(jnp.float32)
    weight_terms = [None] * layers
    small_terms = [None] * layers
    steps = peers.bit_length() - 1
    for layer_index in reversed(range(layers)):
        inputs, kept, unit, inverse, row_block, pre, hidden = saved[layer_index]
        rounded = gradient.astype(jnp.bfloat16).reshape(-1, channels)
        back_hidden = lax.dot_general(
            rounded, w_out[layer_index], dims_cols, preferred_element_type=jnp.float32
        )
        slope = (back_hidden * gelu_slope(pre)).astype(jnp.bfloat16)
        back_norm = lax.dot_general(
            slope, w_in[layer_index], dims_cols, preferred_element_type=jnp.float32
        )
        operand_set = (row_block, slope, rounded, hidden)
        weight_terms[layer_index] = halve(pair_term(operand_set), steps)
        scaled_back = back_norm * norm_gain[layer_index]
        gain_term = jnp.sum(back_norm * unit, axis=0)
        first_mean = jnp.mean(scaled_back, axis=-1, keepdims=True)
        second_mean = jnp.mean(scaled_back * unit, axis=-1, keepdims=True)
        back_conv = (inverse * (scaled_back - first_mean - unit * second_mean)).reshape(
            inputs.shape
        )
        centre, outgoing, kernel_term = backward_conv(
            kept, back_conv, slot_index, present, depth_kernel[layer_index], peers * capacity
        )
        small_terms[layer_index] = double(
            jnp.concatenate([kernel_term, gain_term[None]], axis=0), steps
        )
        gradient = collect(gradient, centre, exchange(outgoing, peers), wanted)
    weights_part = jnp.stack(weight_terms, axis=2)
    small = jnp.stack(small_terms)
    kernel_sum, gain_sum = small[:, :-1], small[:, -1]
    grad_tiles = gradient.astype(jnp.bfloat16)
    return (
        grad_tiles,
        weights_part[:, 0] * scale,
        weights_part[:, 1] * scale,
        kernel_sum * scale,
        gain_sum * scale,
    )


def solution(mesh):
    return jax.shard_map(
        body,
        mesh=mesh,
        in_specs=(
            P(("parts", "tile"), None, None, None),
            P(("parts", "tile"), None, None),
            P(("parts", "tile"), None),
            P(("parts", "tile"), None),
            P(),
            P(),
            P(),
            P(),
            P(("parts", "tile"), None, None, None),
        ),
        out_specs=(
            P(("parts", "tile"), None, None, None),
            P(("parts", "tile"), None, None),
            P(("parts", "tile"), None, None),
            P("parts", None, None),
            P("parts", None),
        ),
        check_vma=False,
    )
```

profile of v0, /device:TPU:0, one launch (start us, length us, event | category | flops | bytes accessed | tf_op | source)
XLA Modules:
  0.0 211.7 jit_solution(1257330435075602751)
XLA Ops:
  1.2 1.3 reduce.6
  2.8 0.7 add_add_fusion
  3.7 13.6 %all_to_all.26 = s32[16,1,2]{2,1,0:T(1,128)S(1)} all-to-all(s32[16,1,2]{2,1,0:T(1,128)S(1)} %bitcast.263), channel_id=1, replica_groups=mesh['parts'=2,'tile'=16] {'tile'}, dimensions={0} | all-to-all | bytes 256 | tf_op jit(solution)/shard_map/all_to_all | solution.py:345
  18.1 0.9 copy-done.2
  19.1 1.9 serve.2
  21.0 3.6 %all-to-all-start.1 = ((bf16[16,2,3,16,256]{4,3,2,1,0:T(8,128)(2,1)}), bf16[16,2,3,16,256]{4,3,2,1,0:T(8,128)(2,1)S(1)}, u32[]{:S(2)}, u32[]{:S(2)}) async-start(bf16[16,2,3,16,256]{4,3,2,1,0:T(8,128)(2,1)} %bitcast.1), calls=%async_computation.1 | async-start | bytes 1572864 | tf_op jit(solution)/shard_map/all_to_all | solution.py:330
  24.8 18.4 %all-to-all-done.1 = bf16[16,2,3,16,256]{4,3,2,1,0:T(8,128)(2,1)S(1)} async-done(((bf16[16,2,3,16,256]{4,3,2,1,0:T(8,128)(2,1)}), bf16[16,2,3,16,256]{4,3,2,1,0:T(8,128)(2,1)S(1)}, u32[]{:S(2)}, u32[]{:S(2)}) %all-to-all-start.1) | async-done | bytes 786464 | tf_op jit(solution)/shard_map/all_to_all | solution.py:330
  43.3 3.9 %forward_conv.2 = (f32[2,22,24,256]{3,2,1,0:T(8,128)S(1)}, f32[2,16,16,256]{3,2,1,0:T(8,128)S(1)}) custom-call(s32[16]{0:T(128)S(1)} %multiply_add_fusion.slot_ref, s32[16]{0:T(128)S(1)} %reshape.351.present_ref, bf16[2,16,16,256]{3,2,1,0:T(8,128)(2,1)S(1)} %copy-done.3, bf16[32,3,16,256]{3,2,1,0:T(8,128)(2,1)S(1)} %bitcast.236, f32[49,256]{1,0:T(8,128)S(1)} %bitcast.239), custom_call_target="tpu_custom_call" | custom-call | tf_op jit(solution)/shard_map/forward_conv/pallas_call | solution.py:117
  47.6 1.0 multiply_convert_fusion.4
  48.7 3.0 %multiply_convert_fusion.1 = (bf16[512,1024]{1,0:T(8,128)(2,1)S(1)}, f32[512,1024]{1,0:T(8,128)}) fusion(bf16[512,256]{1,0:T(8,128)(2,1)S(1)} %bitcast.254, bf16[2,256,1024]{2,1,0:T(8,128)(2,1)} %param.16), kind=kOutput, calls=%fused_computation.18 | convolution fusion | flops 271056896 | bytes 3932160 | tf_op jit(solution)/shard_map/dot_general | solution.py:357
  51.7 1.0 copy-done.15
  53.1 2.0 serve.3
  55.1 5.4 %all-to-all-start.2 = ((bf16[16,2,3,16,256]{4,3,2,1,0:T(8,128)(2,1)}), bf16[16,2,3,16,256]{4,3,2,1,0:T(8,128)(2,1)S(1)}, u32[]{:S(2)}, u32[]{:S(2)}) async-start(bf16[16,2,3,16,256]{4,3,2,1,0:T(8,128)(2,1)} %bitcast.11), calls=%async_computation.2 | async-start | bytes 1572864 | tf_op jit(solution)/shard_map/all_to_all | solution.py:330
  60.6 18.7 %all-to-all-done.2 = bf16[16,2,3,16,256]{4,3,2,1,0:T(8,128)(2,1)S(1)} async-done(((bf16[16,2,3,16,256]{4,3,2,1,0:T(8,128)(2,1)}), bf16[16,2,3,16,256]{4,3,2,1,0:T(8,128)(2,1)S(1)}, u32[]{:S(2)}, u32[]{:S(2)}) %all-to-all-start.2) | async-done | bytes 786464 | tf_op jit(solution)/shard_map/all_to_all | solution.py:330
  79.2 4.0 %forward_conv.3 = (f32[2,22,24,256]{3,2,1,0:T(8,128)S(1)}, f32[2,16,16,256]{3,2,1,0:T(8,128)S(1)}) custom-call(s32[16]{0:T(128)S(1)} %multiply_add_fusion.slot_ref, s32[16]{0:T(128)S(1)} %reshape.351.present_ref, bf16[2,16,16,256]{3,2,1,0:T(8,128)(2,1)S(1)} %fusion.10.inputs_ref, bf16[32,3,16,256]{3,2,1,0:T(8,128)(2,1)S(1)} %bitcast.235, f32[49,256]{1,0:T(8,128)S(1)} %bitcast.241), custom_call_target="tpu_custom_call" | custom-call | tf_op jit(solution)/shard_map/forward_conv/pallas_call | solution.py:117
  83.2 1.0 copy-done
  84.7 1.0 multiply_convert_fusion.3
  85.7 1.5 fusion.33
  87.2 1.9 fusion.4
  89.2 0.9 fusion.11
  90.2 1.9 convolution_bitcast_fusion
  92.2 1.2 fusion.21
  93.6 1.3 fusion.30
  95.0 1.4 fusion.29
  96.4 11.0 %backward_conv.2 = (f32[2,16,16,256]{3,2,1,0:T(8,128)S(1)}, bf16[32,3,16,256]{3,2,1,0:T(8,128)(2,1)}, f32[49,256]{1,0:T(8,128)S(1)}) custom-call(s32[16]{0:T(128)S(1)} %copy-done.7, s32[16]{0:T(128)S(1)} %copy-done.10, f32[2,22,24,256]{3,2,1,0:T(8,128)S(1)} %copy-done.1, f32[2,16,16,256]{3,2,1,0:T(8,128)S(1)} %bitcast.238, f32[49,256]{1,0:T(8,128)S(1)} %bitcast.242), custom_call_target="tpu_custom_call" | custom-call | tf_op jit(solution)/shard_map/backward_conv/pallas_call | solution.py:219
  107.4 5.5 %all-to-all-start.3 = ((bf16[16,2,3,16,256]{4,3,2,1,0:T(8,128)(2,1)}), bf16[16,2,3,16,256]{4,3,2,1,0:T(8,128)(2,1)S(1)}, u32[]{:S(2)}, u32[]{:S(2)}) async-start(bf16[16,2,3,16,256]{4,3,2,1,0:T(8,128)(2,1)} %bitcast.21), calls=%async_computation.3 | async-start | bytes 1572864 | tf_op jit(solution)/shard_map/all_to_all | solution.py:330
  113.0 1.9 bitcast_add_fusion
  115.0 0.8 copy-done.14
  115.8 0.8 fusion.49
  116.6 1.9 collective-permute-start.5
  118.6 10.2 %collective-permute-done.5 = bf16[4,16,2,1024]{3,1,2,0:T(8,128)(2,1)} collective-permute-done((bf16[4,16,2,1024]{3,1,2,0:T(8,128)(2,1)}, bf16[4,16,2,1024]{3,1,2,0:T(8,128)(2,1)}, u32[]{:S(2)}, u32[]{:S(2)}) %collective-permute-start.5) | collective-permute-done | bytes 262176 | tf_op jit(solution)/shard_map/ppermute | solution.py:316
  128.7 1.2 bitcast_add_fusion.1
  130.0 0.8 fusion.56
  130.8 3.0 %collective-permute-start.6 = (bf16[2,16,2,1024]{3,1,2,0:T(8,128)(2,1)}, bf16[2,16,2,1024]{3,1,2,0:T(8,128)(2,1)}, u32[]{:S(2)}, u32[]{:S(2)}) collective-permute-start(bf16[2,16,2,1024]{3,1,2,0:T(8,128)(2,1)} %fusion.56), channel_id=1, source_target_pairs={{0,4},{1,5},{2,6},{3,7},{4,0},{5,1},{6,2},{7,3},{8,12},{9,13},{10,... | collective-permute-start | bytes 393224 | tf_op jit(solution)/shard_map/ppermute | solution.py:316
  133.7 1.1 collective-permute-start.13
  134.9 3.1 %collective-permute-done.13 = f32[50,256]{1,0:T(8,128)S(1)} collective-permute-done((f32[50,256]{1,0:T(8,128)S(1)}, f32[50,256]{1,0:T(8,128)S(1)}, u32[]{:S(2)}, u32[]{:S(2)}) %collective-permute-start.13) | collective-permute-done | bytes 51232 | tf_op jit(solution)/shard_map/ppermute | solution.py:324
  138.1 1.0 convert_element_type.127.base_ref
  139.2 0.8 copy.85
  140.0 2.2 %collective-permute-done.14 = f32[50,256]{1,0:T(8,128)S(1)} collective-permute-done((f32[50,256]{1,0:T(8,128)S(1)}, f32[50,256]{1,0:T(8,128)S(1)}, u32[]{:S(2)}, u32[]{:S(2)}) %collective-permute-start.14) | collective-permute-done | bytes 51232 | tf_op jit(solution)/shard_map/ppermute | solution.py:324
  142.9 1.3 collective-permute-start.15
  144.2 1.8 fusion.53
  146.0 1.2 collect.2.base_ref
  147.9 1.1 fusion.9
  149.1 1.0 copy-done.26
  150.0 1.3 fusion.26
  151.3 1.8 copy.86
  153.2 1.5 convolution_bitcast_fusion.1
  156.0 11.0 %backward_conv.3 = (f32[2,16,16,256]{3,2,1,0:T(8,128)S(1)}, bf16[32,3,16,256]{3,2,1,0:T(8,128)(2,1)}, f32[49,256]{1,0:T(8,128)S(1)}) custom-call(s32[16]{0:T(128)S(1)} %copy-done.8, s32[16]{0:T(128)S(1)} %copy-done.11, f32[2,22,24,256]{3,2,1,0:T(8,128)S(1)} %get-tuple-element.20.padded_ref, f32[2,16,16,256]{3,2,1,0:T(8,128)S(1)} %bitcast.237, ...), custom_call_target="tpu_custom_call" | custom-call | tf_op jit(solution)/shard_map/backward_conv/pallas_call | solution.py:219
  167.3 1.7 collective-permute-start.7
  169.0 1.1 collective-permute-start.9
  170.6 1.0 collective-permute-start.1
  171.6 0.9 add_bitcast_fusion
  172.4 1.1 collective-permute-done.9
  174.0 4.9 %all-to-all-start.4 = ((bf16[16,2,3,16,256]{4,3,2,1,0:T(8,128)(2,1)}), bf16[16,2,3,16,256]{4,3,2,1,0:T(8,128)(2,1)S(1)}, u32[]{:S(2)}, u32[]{:S(2)}) async-start(bf16[16,2,3,16,256]{4,3,2,1,0:T(8,128)(2,1)} %bitcast.26), calls=%async_computation.4 | async-start | bytes 1572864 | tf_op jit(solution)/shard_map/all_to_all | solution.py:330
  178.9 2.9 %collective-permute-start.11 = (f32[50,256]{1,0:T(8,128)S(1)}, f32[50,256]{1,0:T(8,128)S(1)}, u32[]{:S(2)}, u32[]{:S(2)}) collective-permute-start(f32[50,256]{1,0:T(8,128)S(1)} %add.145), channel_id=1, source_target_pairs={{0,8},{1,9},{2,10},{3,11},{4,12},{5,13},{6,14},{7,15},{8,0},{9,1},... | collective-permute-start | bytes 153608 | tf_op jit(solution)/shard_map/ppermute | solution.py:324
  181.8 1.1 bitcast_add_fusion.2
  182.9 1.5 collective-permute-start.2
  184.4 17.8 %collective-permute-done.11 = f32[50,256]{1,0:T(8,128)S(1)} collective-permute-done((f32[50,256]{1,0:T(8,128)S(1)}, f32[50,256]{1,0:T(8,128)S(1)}, u32[]{:S(2)}, u32[]{:S(2)}) %collective-permute-start.11) | collective-permute-done | bytes 51232 | tf_op jit(solution)/shard_map/ppermute | solution.py:324
  203.1 0.7 copy.106
  203.8 4.4 %collective-permute-done.3 = bf16[1,16,2,1024]{3,1,2,0:T(8,128)(2,1)S(1)} collective-permute-done((bf16[1,16,2,1024]{3,1,2,0:T(8,128)(2,1)S(1)}, bf16[1,16,2,1024]{3,1,2,0:T(8,128)(2,1)S(1)}, u32[]{:S(2)}, u32[]{:S(2)}) %collective-permute-start.3) | collective-permute-done | bytes 65568 | tf_op jit(solution)/shard_map/ppermute | solution.py:316
  208.3 0.8 copy.104
  209.0 0.8 copy.105
  209.8 1.2 collect.3
  210.9 0.7 convert_element_type.136
  (151 shorter events, 8.7 us)
Async XLA Ops:
  0.6 24.0 %copy-start.39 = (s32[2,8]{1,0:T(2,128)S(1)}, s32[2,8]{1,0:T(2,128)}, u32[]{:S(2)}) copy-start(s32[2,8]{1,0:T(2,128)} %param.13) | copy-start | bytes 196
  0.6 24.2 %copy-start.35 = (f32[2,256]{1,0:T(2,128)S(1)}, f32[2,256]{1,0:T(2,128)}, u32[]{:S(2)}) copy-start(f32[2,256]{1,0:T(2,128)} %param.15) | copy-start | bytes 6148
  2.8 76.5 %copy-start.6 = (s32[16]{0:T(128)}, s32[16]{0:T(128)S(1)}, u32[]{:S(2)}) copy-start(s32[16]{0:T(128)S(1)} %multiply_add_fusion.slot_ref) | copy-start | bytes 196
  18.1 1.0 copy-start.2
  19.1 34.1 %copy-start.4 = (s32[32]{0:T(128)}, s32[32]{0:T(128)S(1)}, u32[]{:S(2)}) copy-start(s32[32]{0:T(128)S(1)} %reshape.350.wanted_ref) | copy-start | bytes 388
  19.1 5.7 %copy-start.34 = (f32[2,49,256]{2,0,1:T(2,128)S(1)}, f32[2,49,256]{2,0,1:T(2,128)}, u32[]{:S(2)}) copy-start(f32[2,49,256]{2,0,1:T(2,128)} %param.14) | copy-start | bytes 301060
  19.1 24.2 %copy-start.3 = (bf16[2,16,16,256]{3,2,1,0:T(8,128)(2,1)S(1)}, bf16[2,16,16,256]{3,2,1,0:T(8,128)(2,1)}, u32[]{:S(2)}) copy-start(bf16[2,16,16,256]{3,2,1,0:T(8,128)(2,1)} %inputs_ref.3) | copy-start | bytes 786436
  21.0 22.3 %all-to-all-start.1 = ((bf16[16,2,3,16,256]{4,3,2,1,0:T(8,128)(2,1)}), bf16[16,2,3,16,256]{4,3,2,1,0:T(8,128)(2,1)S(1)}, u32[]{:S(2)}, u32[]{:S(2)}) async-start(bf16[16,2,3,16,256]{4,3,2,1,0:T(8,128)(2,1)} %bitcast.1), calls=%async_computation.1 | async-start | bytes 1572864 | tf_op jit(solution)/shard_map/all_to_all | solution.py:330
  24.7 54.5 %copy-start.9 = (s32[16]{0:T(128)}, s32[16]{0:T(128)S(1)}, u32[]{:S(2)}) copy-start(s32[16]{0:T(128)S(1)} %reshape.351.present_ref) | copy-start | bytes 196
  48.7 3.0 %copy-start.18 = (bf16[2,16,16,256]{3,2,1,0:T(8,128)(2,1)}, bf16[2,16,16,256]{3,2,1,0:T(8,128)(2,1)S(1)}, u32[]{:S(2)}) copy-start(bf16[2,16,16,256]{3,2,1,0:T(8,128)(2,1)S(1)} %get-tuple-element.53) | copy-start | bytes 786436
  48.7 4.0 %copy-start.36 = (bf16[2,1024,256]{2,1,0:T(8,128)(2,1)S(1)}, bf16[2,1024,256]{2,1,0:T(8,128)(2,1)}, u32[]{:S(2)}) copy-start(bf16[2,1024,256]{2,1,0:T(8,128)(2,1)} %param.17) | copy-start | bytes 3145732
  51.7 1.0 copy-start.15
  55.1 24.1 %all-to-all-start.2 = ((bf16[16,2,3,16,256]{4,3,2,1,0:T(8,128)(2,1)}), bf16[16,2,3,16,256]{4,3,2,1,0:T(8,128)(2,1)S(1)}, u32[]{:S(2)}, u32[]{:S(2)}) async-start(bf16[16,2,3,16,256]{4,3,2,1,0:T(8,128)(2,1)} %bitcast.11), calls=%async_computation.2 | async-start | bytes 1572864 | tf_op jit(solution)/shard_map/all_to_all | solution.py:330
  83.2 1.0 copy-start
  84.7 2.5 %copy-start.32 = (bf16[2,16,16,256]{3,2,1,0:T(8,128)(2,1)S(1)}, bf16[2,16,16,256]{3,2,1,0:T(8,128)(2,1)}, u32[]{:S(2)}) copy-start(bf16[2,16,16,256]{3,2,1,0:T(8,128)(2,1)} %param.18) | copy-start | bytes 786436
  84.7 2.5 %copy-start.37 = (bf16[2,1024,256]{2,1,0:T(8,128)(2,1)S(1)}, bf16[2,1024,256]{2,1,0:T(8,128)(2,1)}, u32[]{:S(2)}) copy-start(bf16[2,1024,256]{2,1,0:T(8,128)(2,1)} %param.17) | copy-start | bytes 3145732
  90.0 3.3 %copy-start.12 = (f32[1024,256]{0,1:T(8,128)}, f32[1024,256]{0,1:T(8,128)S(1)}, u32[]{:S(2)}) copy-start(f32[1024,256]{0,1:T(8,128)S(1)} %fusion.11) | copy-start | bytes 3145732
  90.2 3.4 %copy-start.21 = (f32[2,16,16,256]{3,2,1,0:T(8,128)S(1)}, f32[2,16,16,256]{3,2,1,0:T(8,128)}, u32[]{:S(2)}) copy-start(f32[2,16,16,256]{3,2,1,0:T(8,128)} %get-tuple-element.52) | copy-start | bytes 1572868
  90.2 3.4 %copy-start.29 = (bf16[2,256,1024]{2,1,0:T(8,128)(2,1)S(1)}, bf16[2,256,1024]{2,1,0:T(8,128)(2,1)}, u32[]{:S(2)}) copy-start(bf16[2,256,1024]{2,1,0:T(8,128)(2,1)} %param.16) | copy-start | bytes 3145732
  90.2 3.4 %copy-start.31 = (bf16[512,1024]{1,0:T(8,128)(2,1)S(1)}, bf16[512,1024]{1,0:T(8,128)(2,1)}, u32[]{:S(2)}) copy-start(bf16[512,1024]{1,0:T(8,128)(2,1)} %fusion.4) | copy-start | bytes 3145732
  92.2 1.4 copy-start.13
  93.3 19.6 %collective-permute-start.4 = (bf16[8,16,2,1024]{3,1,0,2:T(8,128)(2,1)}, bf16[8,16,2,1024]{3,1,0,2:T(8,128)(2,1)}, u32[]{:S(2)}, u32[]{:S(2)}) collective-permute-start(bf16[8,16,2,1024]{3,1,0,2:T(8,128)(2,1)} %fusion.21), channel_id=1, source_target_pairs={{0,1},{1,0},{2,3},{3,2},{4,5},{5,4},{6,7},{7,6},{8,9},{9,8},{10,11... | collective-permute-start | bytes 1572872 | tf_op jit(solution)/shard_map/ppermute | solution.py:316
  93.6 1.4 copy-start.22
  93.6 2.8 %copy-start.1 = (f32[2,22,24,256]{3,2,1,0:T(8,128)S(1)}, f32[2,22,24,256]{3,2,1,0:T(8,128)}, u32[]{:S(2)}) copy-start(f32[2,22,24,256]{3,2,1,0:T(8,128)} %copy-done) | copy-start | bytes 3244036
  93.6 2.8 %copy-start.7 = (s32[16]{0:T(128)S(1)}, s32[16]{0:T(128)}, u32[]{:S(2)}) copy-start(s32[16]{0:T(128)} %copy-done.6) | copy-start | bytes 196
  93.6 2.8 %copy-start.10 = (s32[16]{0:T(128)S(1)}, s32[16]{0:T(128)}, u32[]{:S(2)}) copy-start(s32[16]{0:T(128)} %copy-done.9) | copy-start | bytes 196
  107.4 38.6 %all-to-all-start.3 = ((bf16[16,2,3,16,256]{4,3,2,1,0:T(8,128)(2,1)}), bf16[16,2,3,16,256]{4,3,2,1,0:T(8,128)(2,1)S(1)}, u32[]{:S(2)}, u32[]{:S(2)}) async-start(bf16[16,2,3,16,256]{4,3,2,1,0:T(8,128)(2,1)} %bitcast.21), calls=%async_computation.3 | async-start | bytes 1572864 | tf_op jit(solution)/shard_map/all_to_all | solution.py:330
  115.0 0.8 copy-start.14
  115.8 23.4 %copy-start.19 = (bf16[2,16,16,256]{3,2,1,0:T(8,128)(2,1)S(1)}, bf16[2,16,16,256]{3,2,1,0:T(8,128)(2,1)}, u32[]{:S(2)}) copy-start(bf16[2,16,16,256]{3,2,1,0:T(8,128)(2,1)} %copy-done.18) | copy-start | bytes 786436
  116.6 12.2 %collective-permute-start.5 = (bf16[4,16,2,1024]{3,1,2,0:T(8,128)(2,1)}, bf16[4,16,2,1024]{3,1,2,0:T(8,128)(2,1)}, u32[]{:S(2)}, u32[]{:S(2)}) collective-permute-start(bf16[4,16,2,1024]{3,1,2,0:T(8,128)(2,1)} %fusion.49), channel_id=1, source_target_pairs={{0,2},{1,3},{2,0},{3,1},{4,6},{5,7},{6,4},{7,5},{8,10},{9,11},{10,... | collective-permute-start | bytes 786440 | tf_op jit(solution)/shard_map/ppermute | solution.py:316
  118.5 27.5 %copy-start.5 = (s32[32]{0:T(128)S(1)}, s32[32]{0:T(128)}, u32[]{:S(2)}) copy-start(s32[32]{0:T(128)} %copy-done.4) | copy-start | bytes 388
  118.5 15.2 %collective-permute-start.12 = (f32[50,256]{1,0:T(8,128)S(1)}, f32[50,256]{1,0:T(8,128)S(1)}, u32[]{:S(2)}, u32[]{:S(2)}) collective-permute-start(f32[50,256]{1,0:T(8,128)S(1)} %pad_maximum_fusion.4), channel_id=1, source_target_pairs={{0,1},{1,0},{2,3},{3,2},{4,5},{5,4},{6,7},{7,6},{8,9},{9,8},{10,11... | collective-permute-start | bytes 153608 | tf_op jit(solution)/shard_map/ppermute | solution.py:324
  130.0 8.0 %copy-start.17 = (f32[4,16,2,1024]{3,1,2,0:T(8,128)}, f32[4,16,2,1024]{3,1,2,0:T(8,128)S(1)}, u32[]{:S(2)}) copy-start(f32[4,16,2,1024]{3,1,2,0:T(8,128)S(1)} %bitcast_add_fusion.1) | copy-start | bytes 1572868
  130.8 13.4 %collective-permute-start.6 = (bf16[2,16,2,1024]{3,1,2,0:T(8,128)(2,1)}, bf16[2,16,2,1024]{3,1,2,0:T(8,128)(2,1)}, u32[]{:S(2)}, u32[]{:S(2)}) collective-permute-start(bf16[2,16,2,1024]{3,1,2,0:T(8,128)(2,1)} %fusion.56), channel_id=1, source_target_pairs={{0,4},{1,5},{2,6},{3,7},{4,0},{5,1},{6,2},{7,3},{8,12},{9,13},{10,... | collective-permute-start | bytes 393224 | tf_op jit(solution)/shard_map/ppermute | solution.py:316
  133.7 4.2 %collective-permute-start.13 = (f32[50,256]{1,0:T(8,128)S(1)}, f32[50,256]{1,0:T(8,128)S(1)}, u32[]{:S(2)}, u32[]{:S(2)}) collective-permute-start(f32[50,256]{1,0:T(8,128)S(1)} %fusion.84), channel_id=1, source_target_pairs={{0,2},{1,3},{2,0},{3,1},{4,6},{5,7},{6,4},{7,5},{8,10},{9,11},{10,... | collective-permute-start | bytes 153608 | tf_op jit(solution)/shard_map/ppermute | solution.py:324
  138.0 4.2 %collective-permute-start.14 = (f32[50,256]{1,0:T(8,128)S(1)}, f32[50,256]{1,0:T(8,128)S(1)}, u32[]{:S(2)}, u32[]{:S(2)}) collective-permute-start(f32[50,256]{1,0:T(8,128)S(1)} %add.148), channel_id=1, source_target_pairs={{0,4},{1,5},{2,6},{3,7},{4,0},{5,1},{6,2},{7,3},{8,12},{9,13},{10,... | collective-permute-start | bytes 153608 | tf_op jit(solution)/shard_map/ppermute | solution.py:324
  142.9 28.7 %collective-permute-start.15 = (f32[50,256]{1,0:T(8,128)}, f32[50,256]{1,0:T(8,128)}, u32[]{:S(2)}, u32[]{:S(2)}) collective-permute-start(f32[50,256]{1,0:T(8,128)} %add.149), channel_id=1, source_target_pairs={{0,8},{1,9},{2,10},{3,11},{4,12},{5,13},{6,14},{7,15},{8,0},{9,1},... | collective-permute-start | bytes 153608 | tf_op jit(solution)/shard_map/ppermute | solution.py:324
  146.0 1.6 copy-start.23
  146.0 1.9 copy-start.38
  147.3 1.8 copy-start.28
  147.9 2.1 %copy-start.20 = (f32[2,16,16,256]{3,2,1,0:T(8,128)S(1)}, f32[2,16,16,256]{3,2,1,0:T(8,128)}, u32[]{:S(2)}) copy-start(f32[2,16,16,256]{3,2,1,0:T(8,128)} %get-tuple-element.54) | copy-start | bytes 1572868
  147.9 2.1 %copy-start.30 = (bf16[2,256,1024]{2,1,0:T(8,128)(2,1)S(1)}, bf16[2,256,1024]{2,1,0:T(8,128)(2,1)}, u32[]{:S(2)}) copy-start(bf16[2,256,1024]{2,1,0:T(8,128)(2,1)} %param.16) | copy-start | bytes 3145732
  149.0 1.0 copy-start.26
  149.1 4.1 %copy-start.16 = (bf16[512,1024]{1,0:T(8,128)(2,1)S(1)}, bf16[512,1024]{1,0:T(8,128)(2,1)}, u32[]{:S(2)}) copy-start(bf16[512,1024]{1,0:T(8,128)(2,1)} %copy-done.15) | copy-start | bytes 3145732
  151.3 3.4 %copy-start.25 = (bf16[256,512]{1,0:T(8,128)(2,1)S(1)}, bf16[256,512]{1,0:T(8,128)(2,1)}, u32[]{:S(2)}) copy-start(bf16[256,512]{1,0:T(8,128)(2,1)} %copy.85) | copy-start | bytes 786436
  153.1 1.5 copy-start.27
  154.7 1.0 copy-start.33
  155.1 0.8 copy-start.8
  155.2 0.8 copy-start.11
  155.3 11.9 %copy-start.24 = (f32[1,2,16,2,1024]{4,2,3,1,0:T(8,128)S(1)}, f32[1,2,16,2,1024]{4,2,3,1,0:T(8,128)}, u32[]{:S(2)}) copy-start(f32[1,2,16,2,1024]{4,2,3,1,0:T(8,128)} %fusion.53) | copy-start | bytes 786436
  155.3 14.8 %collective-permute-start = (bf16[8,16,2,1024]{3,1,0,2:T(8,128)(2,1)S(1)}, bf16[8,16,2,1024]{3,1,0,2:T(8,128)(2,1)S(1)}, u32[]{:S(2)}, u32[]{:S(2)}) collective-permute-start(bf16[8,16,2,1024]{3,1,0,2:T(8,128)(2,1)S(1)} %fusion.20), channel_id=1, source_target_pairs={{0,1},{1,0},{2,3},{3,2},{4,5},{5,4},{6,7},{7,6},{8,9},{9,8},{10,11... | collective-permute-start | bytes 1572872 | tf_op jit(solution)/shard_map/ppermute | solution.py:316
  167.0 2.0 collective-permute-start.8
  167.3 6.7 %collective-permute-start.7 = (bf16[1,16,2,1024]{3,1,2,0:T(8,128)(2,1)S(1)}, bf16[1,16,2,1024]{3,1,2,0:T(8,128)(2,1)S(1)}, u32[]{:S(2)}, u32[]{:S(2)}) collective-permute-start(bf16[1,16,2,1024]{3,1,2,0:T(8,128)(2,1)S(1)} %fusion.65), channel_id=1, source_target_pairs={{0,8},{1,9},{2,10},{3,11},{4,12},{5,13},{6,14},{7,15},{8,0},{9,1},... | collective-permute-start | bytes 196616 | tf_op jit(solution)/shard_map/ppermute | solution.py:316
  169.0 4.6 %collective-permute-start.9 = (f32[50,256]{1,0:T(8,128)S(1)}, f32[50,256]{1,0:T(8,128)S(1)}, u32[]{:S(2)}, u32[]{:S(2)}) collective-permute-start(f32[50,256]{1,0:T(8,128)S(1)} %fusion.83), channel_id=1, source_target_pairs={{0,2},{1,3},{2,0},{3,1},{4,6},{5,7},{6,4},{7,5},{8,10},{9,11},{10,... | collective-permute-start | bytes 153608 | tf_op jit(solution)/shard_map/ppermute | solution.py:324
  170.6 11.2 %collective-permute-start.1 = (bf16[4,16,2,1024]{3,1,2,0:T(8,128)(2,1)S(1)}, bf16[4,16,2,1024]{3,1,2,0:T(8,128)(2,1)}, u32[]{:S(2)}, u32[]{:S(2)}) collective-permute-start(bf16[4,16,2,1024]{3,1,2,0:T(8,128)(2,1)S(1)} %fusion.48), channel_id=1, source_target_pairs={{0,2},{1,3},{2,0},{3,1},{4,6},{5,7},{6,4},{7,5},{8,10},{9,11},{10,... | collective-permute-start | bytes 786440 | tf_op jit(solution)/shard_map/ppermute | solution.py:316
  173.5 5.3 %collective-permute-start.10 = (f32[50,256]{1,0:T(8,128)S(1)}, f32[50,256]{1,0:T(8,128)S(1)}, u32[]{:S(2)}, u32[]{:S(2)}) collective-permute-start(f32[50,256]{1,0:T(8,128)S(1)} %add.144), channel_id=1, source_target_pairs={{0,4},{1,5},{2,6},{3,7},{4,0},{5,1},{6,2},{7,3},{8,12},{9,13},{10,... | collective-permute-start | bytes 153608 | tf_op jit(solution)/shard_map/ppermute | solution.py:324
  174.0 35.8 %all-to-all-start.4 = ((bf16[16,2,3,16,256]{4,3,2,1,0:T(8,128)(2,1)}), bf16[16,2,3,16,256]{4,3,2,1,0:T(8,128)(2,1)S(1)}, u32[]{:S(2)}, u32[]{:S(2)}) async-start(bf16[16,2,3,16,256]{4,3,2,1,0:T(8,128)(2,1)} %bitcast.26), calls=%async_computation.4 | async-start | bytes 1572864 | tf_op jit(solution)/shard_map/all_to_all | solution.py:330
  178.9 23.4 %collective-permute-start.11 = (f32[50,256]{1,0:T(8,128)S(1)}, f32[50,256]{1,0:T(8,128)S(1)}, u32[]{:S(2)}, u32[]{:S(2)}) collective-permute-start(f32[50,256]{1,0:T(8,128)S(1)} %add.145), channel_id=1, source_target_pairs={{0,8},{1,9},{2,10},{3,11},{4,12},{5,13},{6,14},{7,15},{8,0},{9,1},... | collective-permute-start | bytes 153608 | tf_op jit(solution)/shard_map/ppermute | solution.py:324
  182.9 20.0 %collective-permute-start.2 = (bf16[2,16,2,1024]{3,1,2,0:T(8,128)(2,1)S(1)}, bf16[2,16,2,1024]{3,1,2,0:T(8,128)(2,1)S(1)}, u32[]{:S(2)}, u32[]{:S(2)}) collective-permute-start(bf16[2,16,2,1024]{3,1,2,0:T(8,128)(2,1)S(1)} %fusion.55), channel_id=1, source_target_pairs={{0,4},{1,5},{2,6},{3,7},{4,0},{5,1},{6,2},{7,3},{8,12},{9,13},{10,... | collective-permute-start | bytes 393224 | tf_op jit(solution)/shard_map/ppermute | solution.py:316
  203.0 5.2 %collective-permute-start.3 = (bf16[1,16,2,1024]{3,1,2,0:T(8,128)(2,1)S(1)}, bf16[1,16,2,1024]{3,1,2,0:T(8,128)(2,1)S(1)}, u32[]{:S(2)}, u32[]{:S(2)}) collective-permute-start(bf16[1,16,2,1024]{3,1,2,0:T(8,128)(2,1)S(1)} %fusion.64), channel_id=1, source_target_pairs={{0,8},{1,9},{2,10},{3,11},{4,12},{5,13},{6,14},{7,15},{8,0},{9,1},... | collective-permute-start | bytes 196616 | tf_op jit(solution)/shard_map/ppermute | solution.py:316
where the time goes:
time: 213 us; the launch traced here: 212 us
  waiting for transfers between devices  76.2 us (36%)
  Pallas kernels  36.1 us (17%)
  starting transfers between devices  36.1 us (17%)
  other arithmetic  20.3 us (10%)
  matrix products  15.3 us (7%)
  blocking collectives  13.6 us (6%)
  local copies, waits for them, and re-layouts  12.7 us (6%)
    all_to_all x4, waiting for transfers between devices, exchange(): lax.all_to_all(arranged, 'tile', split_axis=0, concat_axis=0, tiled=True)  37.1 us
    ppermute x8, waiting for transfers between devices, double(): values = values + lax.ppermute(values, 'tile', partners)  24.3 us
    pallas_call x2, Pallas kernels, backward_conv(): pl.pallas_call(backward_kernel, out_shape=(jax.ShapeDtypeStruct(back_conv...  22 us
    all_to_all x4, starting transfers between devices, exchange(): lax.all_to_all(arranged, 'tile', split_axis=0, concat_axis=0, tiled=True)  19.5 us
    ppermute x8, waiting for transfers between devices, halve(): values = kept + lax.ppermute(sent, 'tile', partners).astype(jnp.float32)  14.7 us
    all_to_all x1, blocking collectives, body(): lax.all_to_all(request, 'tile', split_axis=0, concat_axis=0, tiled=True)  13.6 us
    ppermute x8, starting transfers between devices, halve(): values = kept + lax.ppermute(sent, 'tile', partners).astype(jnp.float32)  9.49 us
    unnamed x87, local copies, waits for them, and re-layouts  9.05 us
  transfers between devices with their start and end apart: 20, of which 9 were waited for; matrix products, arithmetic and copies ran while one was open for 11% of the time, Pallas kernels for 11%

commit v1 on v0

--- a/solution.py
+++ b/solution.py
@@ -1,3 +1,4 @@
+import functools
 import math
 
 import jax
@@ -26,6 +27,73 @@
 LANES = 128
 SMEM = pl.BlockSpec(memory_space=pltpu.SMEM)
 VMEM = pl.BlockSpec(memory_space=pltpu.VMEM)
+
+
+def estimate(microseconds):
+    return pl.CostEstimate(
+        flops=int(microseconds * 1.1e9), bytes_accessed=int(microseconds * 3.6e6), transcendentals=0
+    )
+
+
+def exchange_kernel(peers, source_ref, target_ref, send_sem, recv_sem, own_sem):
+    me = lax.axis_index("tile")
+    barrier = pltpu.get_barrier_semaphore()
+
+    def greet(offset, carry):
+        pl.semaphore_signal(
+            barrier,
+            inc=1,
+            device_id={"tile": lax.rem(me + offset, peers)},
+            device_id_type=pl.DeviceIdType.MESH,
+        )
+        return carry
+
+    def remote(offset):
+        other = lax.rem(me + offset, peers)
+        return pltpu.make_async_remote_copy(
+            src_ref=source_ref.at[other],
+            dst_ref=target_ref.at[me],
+            send_sem=send_sem.at[offset],
+            recv_sem=recv_sem.at[offset],
+            device_id={"tile": other},
+            device_id_type=pl.DeviceIdType.MESH,
+        )
+
+    def begin(offset, carry):
+        remote(offset).start()
+        return carry
+
+    def finish(offset, carry):
+        remote(offset).wait()
+        return carry
+
+    lax.fori_loop(1, peers, greet, 0)
+    pl.semaphore_wait(barrier, peers - 1)
+    lax.fori_loop(1, peers, begin, 0)
+    own = pltpu.make_async_copy(source_ref.at[me], target_ref.at[me], own_sem)
+    own.start()
+    lax.fori_loop(1, peers, finish, 0)
+    own.wait()
+
+
+def direct_exchange(blocks, peers, identity):
+    arranged = blocks.reshape((peers, -1) + blocks.shape[1:])
+    returned = pl.pallas_call(
+        functools.partial(exchange_kernel, peers),
+        out_shape=jax.ShapeDtypeStruct(arranged.shape, arranged.dtype),
+        in_specs=[VMEM],
+        out_specs=VMEM,
+        scratch_shapes=[
+            pltpu.SemaphoreType.DMA((peers,)),
+            pltpu.SemaphoreType.DMA((peers,)),
+            pltpu.SemaphoreType.DMA,
+        ],
+        compiler_params=pltpu.CompilerParams(
+            collective_id=identity, has_side_effects=True, vmem_limit_bytes=16 * 1024 * 1024
+        ),
+        name="exchange_requests" if identity == 0 else "exchange_strips",
+    )(arranged)
+    return returned.reshape(blocks.shape)
 
 
 def serve_kernel(wanted_ref, inputs_ref, out_ref, wide_ref, table_ref):
@@ -131,17 +199,10 @@
     )(slot_index, present, inputs, incoming, kernel)
 
 
-def backward_kernel(
-    slot_ref, present_ref, padded_ref, slopes_ref, kernel_ref,
-    centre_ref, outgoing_ref, taps_ref, piece_ref, shifted_ref, border_ref, sums_ref, back_ref,
-):
+def taps_kernel(padded_ref, slopes_ref, taps_ref, shifted_ref, sums_ref):
     channels = slopes_ref.shape[3]
-    outgoing_ref[...] = jnp.zeros(outgoing_ref.shape, outgoing_ref.dtype)
-    border_ref[...] = jnp.zeros(border_ref.shape, jnp.float32)
     for tile in range(slopes_ref.shape[0]):
         shift_columns(padded_ref, tile, shifted_ref)
-        for tap_col in range(7):
-            border_ref[tap_col, 6:22, tap_col : tap_col + 16, :] = slopes_ref[tile]
         for half in range(channels // LANES):
             lanes = pl.ds(half * LANES, LANES)
 
@@ -170,6 +231,42 @@
                 return carry
 
             lax.fori_loop(0, 7, taps, 0)
+    for tap_col in range(7):
+        for tap_row in range(7):
+            taps_ref[pl.ds(7 * tap_row + tap_col, 1)] = jnp.sum(
+                sums_ref[tap_col, tap_row], axis=0, keepdims=True
+            )
+
+
+def tap_sums(padded, back_conv):
+    _, extent, _, channels = back_conv.shape
+    return pl.pallas_call(
+        taps_kernel,
+        out_shape=jax.ShapeDtypeStruct((49, channels), jnp.float32),
+        in_specs=[VMEM, VMEM],
+        out_specs=VMEM,
+        scratch_shapes=[
+            pltpu.VMEM((7, extent + 6, extent, channels), jnp.float32),
+            pltpu.VMEM((7, 7, extent, channels), jnp.float32),
+        ],
+        compiler_params=pltpu.CompilerParams(vmem_limit_bytes=32 * 1024 * 1024),
+        cost_estimate=estimate(5),
+        name="tap_sums",
+    )(padded, back_conv)
+
+
+def backward_kernel(
+    slot_ref, present_ref, slopes_ref, kernel_ref,
+    centre_ref, outgoing_ref, piece_ref, border_ref, back_ref,
+):
+    channels = slopes_ref.shape[3]
+    outgoing_ref[...] = jnp.zeros(outgoing_ref.shape, outgoing_ref.dtype)
+    border_ref[...] = jnp.zeros(border_ref.shape, jnp.float32)
+    for tile in range(slopes_ref.shape[0]):
+        for tap_col in range(7):
+            border_ref[tap_col, 6:22, tap_col : tap_col + 16, :] = slopes_ref[tile]
+        for half in range(channels // LANES):
+            lanes = pl.ds(half * LANES, LANES)
 
             def rows_back(step, carry):
                 top = step * 2
@@ -207,34 +304,27 @@
             piece_ref[...] = jnp.zeros(piece_ref.shape, jnp.float32)
             piece_ref[:, taken : taken + 3, :] = back_ref[top : top + 3, left : left + 3, :]
             send(direction)
-    for tap_col in range(7):
-        for tap_row in range(7):
-            taps_ref[pl.ds(7 * tap_row + tap_col, 1)] = jnp.sum(
-                sums_ref[tap_col, tap_row], axis=0, keepdims=True
-            )
-
-
-def backward_conv(padded, back_conv, slot_index, present, kernel, slots):
-    tiles, extent, _, channels = back_conv.shape
+
+
+def backward_conv(back_conv, slot_index, present, kernel, slots):
+    _, extent, _, channels = back_conv.shape
     return pl.pallas_call(
         backward_kernel,
         out_shape=(
             jax.ShapeDtypeStruct(back_conv.shape, jnp.float32),
             jax.ShapeDtypeStruct((slots, 3, extent, channels), jnp.bfloat16),
-            jax.ShapeDtypeStruct((49, channels), jnp.float32),
         ),
-        in_specs=[SMEM, SMEM, VMEM, VMEM, VMEM],
-        out_specs=(VMEM, VMEM, VMEM),
+        in_specs=[SMEM, SMEM, VMEM, VMEM],
+        out_specs=(VMEM, VMEM),
         scratch_shapes=[
             pltpu.VMEM((3, extent, channels), jnp.float32),
-            pltpu.VMEM((7, extent + 6, extent, channels), jnp.float32),
             pltpu.VMEM((7, extent + 12, extent + 8, channels), jnp.float32),
-            pltpu.VMEM((7, 7, extent, channels), jnp.float32),
             pltpu.VMEM((extent + 6, extent + 8, channels), jnp.float32),
         ],
-        compiler_params=pltpu.CompilerParams(vmem_limit_bytes=48 * 1024 * 1024),
+        compiler_params=pltpu.CompilerParams(vmem_limit_bytes=32 * 1024 * 1024),
+        cost_estimate=estimate(7),
         name="backward_conv",
-    )(slot_index, present, padded, back_conv, kernel)
+    )(slot_index, present, back_conv, kernel)
 
 
 def collect_kernel(wanted_ref, base_ref, centre_ref, returned_ref, out_ref, table_ref):
@@ -342,13 +432,15 @@
     capacity = max(2, 2 * ((8 * local_tiles + peers - 1) // peers))
     scale = 1.0 / math.sqrt(local_tiles * peers * extent * extent)
     slot_index, request = build_routes(source_device, source_slot, peers, capacity)
-    wanted = lax.all_to_all(request, "tile", split_axis=0, concat_axis=0, tiled=True).reshape(-1)
+    framed = jnp.pad(request[:, None, :], ((0, 0), (0, 7), (0, 128 - capacity)))
+    wanted = direct_exchange(framed.reshape(peers * 8, 128), peers, 0)
+    wanted = wanted.reshape(peers, 8, 128)[:, 0, :capacity].reshape(-1)
     present = present.reshape(-1)
     dims_cols = (((1,), (1,)), ((), ()))
     saved = []
     current = tiles
     for layer_index in range(layers):
-        incoming = exchange(serve(current, wanted), peers)
+        incoming = direct_exchange(serve(current, wanted), peers, 1)
         padded, conv = forward_conv(
             current, incoming, slot_index, present, depth_kernel[layer_index]
         )
@@ -385,7 +477,6 @@
             slope, w_in[layer_index], dims_cols, preferred_element_type=jnp.float32
         )
         operand_set = (row_block, slope, rounded, hidden)
-        weight_terms[layer_index] = halve(pair_term(operand_set), steps)
         scaled_back = back_norm * norm_gain[layer_index]
         gain_term = jnp.sum(back_norm * unit, axis=0)
         first_mean = jnp.mean(scaled_back, axis=-1, keepdims=True)
@@ -393,9 +484,14 @@
         back_conv = (inverse * (scaled_back - first_mean - unit * second_mean)).reshape(
             inputs.shape
         )
-        centre, outgoing, kernel_term = backward_conv(
-            kept, back_conv, slot_index, present, depth_kernel[layer_index], peers * capacity
-        )
+        centre, outgoing = backward_conv(
+            back_conv, slot_index, present, depth_kernel[layer_index], peers * capacity
+        )
+        if layer_index > 0:
+            outgoing, back_conv, slope = lax.optimization_barrier((outgoing, back_conv, slope))
+            operand_set = (row_block, slope, rounded, hidden)
+        weight_terms[layer_index] = halve(pair_term(operand_set), steps)
+        kernel_term = tap_sums(kept, back_conv)
         small_terms[layer_index] = double(
             jnp.concatenate([kernel_term, gain_term[None]], axis=0), steps
         )

time: 213 us -> 199 us (0.934)
  Pallas kernels: 36.1 us -> 86 us
  waiting for transfers between devices: 76.2 us -> 41.8 us
  blocking collectives: 13.6 us -> 0 us
  starting transfers between devices: 36.1 us -> 29.1 us
  other arithmetic: 20.3 us -> 14 us
    pallas_call x0 -> x5, Pallas kernels: none -> 55.2 us  [the longest x3 48.2 us: direct_exchange(): pl.pallas_call(functools.partial(exchange_kernel, peers), out_shape=jax.S...]
    all_to_all x4 -> x2, waiting for transfers between devices: 37.1 us -> 0.01 us  [exchange(): lax.all_to_all(arranged, 'tile', split_axis=0, concat_axis=0, tiled=True)]
    all_to_all x1 -> x0, blocking collectives: 13.6 us -> none  [body(): lax.all_to_all(request, 'tile', split_axis=0, concat_axis=0, tiled=True)]
    ppermute x8, waiting for transfers between devices: 24.3 us -> 31.1 us  [double(): values = values + lax.ppermute(values, 'tile', partners)]
    all_to_all x4 -> x2, starting transfers between devices: 19.5 us -> 13.1 us  [exchange(): lax.all_to_all(arranged, 'tile', split_axis=0, concat_axis=0, tiled=True)]
    pallas_call x2, Pallas kernels: 22 us -> 17.6 us  [backward_conv(): pl.pallas_call(backward_kernel, out_shape=(jax.ShapeDtypeStruct(back_conv...]
    ppermute x8, waiting for transfers between devices: 14.7 us -> 10.7 us  [halve(): values = kept + lax.ppermute(sent, 'tile', partners).astype(jnp.float32)]
    dot_general x2, matrix products: 2.35 us -> 5.08 us  [pair_term(): lax.dot_general(rounded, hidden, dims_rows, preferred_element_type=jnp.fl...]
  transfers between devices with their start and end apart: 20 -> 18, of which waited for: 9 -> 7; matrix products, arithmetic and copies ran while one was open for 11% -> 9% of each run, Pallas kernels for 11% -> 6%
where the time goes in v1:
time: 199 us; the launch traced here: 198 us
  Pallas kernels  86 us (43%)
  waiting for transfers between devices  41.8 us (21%)
  starting transfers between devices  29.1 us (15%)
  other arithmetic  14 us (7%)
  matrix products  13.5 us (7%)
  local copies, waits for them, and re-layouts  12.5 us (6%)
    pallas_call x3, Pallas kernels, direct_exchange(): pl.pallas_call(functools.partial(exchange_kernel, peers), out_shape=jax.S...  48.2 us
    ppermute x8, waiting for transfers between devices, double(): values = values + lax.ppermute(values, 'tile', partners)  31.1 us
    pallas_call x2, Pallas kernels, backward_conv(): pl.pallas_call(backward_kernel, out_shape=(jax.ShapeDtypeStruct(back_conv...  17.6 us
    all_to_all x2, starting transfers between devices, exchange(): lax.all_to_all(arranged, 'tile', split_axis=0, concat_axis=0, tiled=True)  13.1 us
    ppermute x8, waiting for transfers between devices, halve(): values = kept + lax.ppermute(sent, 'tile', partners).astype(jnp.float32)  10.7 us
    ppermute x8, starting transfers between devices, halve(): values = kept + lax.ppermute(sent, 'tile', partners).astype(jnp.float32)  8.84 us
    pallas_call x2, Pallas kernels, forward_conv(): pl.pallas_call(forward_kernel, out_shape=(jax.ShapeDtypeStruct((tiles, ex...  8.77 us
    unnamed x61, local copies, waits for them, and re-layouts  8.05 us
  transfers between devices with their start and end apart: 18, of which 7 were waited for; matrix products, arithmetic and copies ran while one was open for 9% of the time, Pallas kernels for 6%

profile of v1, /device:TPU:0, one launch (start us, length us, event | category | flops | bytes accessed | tf_op | source)
XLA Modules:
  0.0 198.3 jit_solution(6238768710317130351)
XLA Ops:
  0.6 0.8 reshape.342.present_ref
  1.4 0.5 broadcast.272
  2.0 1.3 reduce.7
  3.6 0.7 add_add_fusion
  4.4 0.8 fusion.72
  5.3 9.1 %exchange_requests.1 = s32[16,8,128]{2,1,0:T(8,128)S(1)} custom-call(s32[16,8,128]{2,1,0:T(8,128)S(1)} %pad.4.source_ref), custom_call_target="tpu_custom_call" | custom-call | tf_op jit(solution)/shard_map/exchange_requests/pallas_call | solution.py:81
  14.5 1.1 fusion.71
  15.6 0.9 copy-done
  16.5 1.1 serve.2
  17.6 17.6 %exchange_strips.2 = bf16[16,2,3,16,256]{4,3,2,1,0:T(8,128)(2,1)S(1)} custom-call(bf16[16,2,3,16,256]{4,3,2,1,0:T(8,128)(2,1)S(1)} %bitcast.235), custom_call_target="tpu_custom_call" | custom-call | tf_op jit(solution)/shard_map/exchange_strips/pallas_call | solution.py:81
  35.3 4.2 %forward_conv.2 = (f32[2,22,24,256]{3,2,1,0:T(8,128)S(1)}, f32[2,16,16,256]{3,2,1,0:T(8,128)S(1)}) custom-call(s32[16]{0:T(128)S(1)} %multiply_add_fusion.slot_ref, s32[16]{0:T(128)S(1)} %reshape.342.present_ref, bf16[2,16,16,256]{3,2,1,0:T(8,128)(2,1)S(1)} %copy-done.1, bf16[32,3,16,256]{3,2,1,0:T(8,128)(2,1)S(1)} %bitcast.233, ...), custom_call_target="tpu_custom_call" | custom-call | tf_op jit(solution)/shard_map/forward_conv/pallas_call | solution.py:185
  39.9 1.0 multiply_convert_fusion.4
  40.9 1.8 multiply_convert_fusion.1
  42.8 1.0 copy-done.9
  44.2 1.1 serve.3
  45.3 21.6 %exchange_strips.3 = bf16[16,2,3,16,256]{4,3,2,1,0:T(8,128)(2,1)S(1)} custom-call(bf16[16,2,3,16,256]{4,3,2,1,0:T(8,128)(2,1)S(1)} %bitcast.236), custom_call_target="tpu_custom_call" | custom-call | tf_op jit(solution)/shard_map/exchange_strips/pallas_call | solution.py:81
  66.8 4.5 %forward_conv.3 = (f32[2,22,24,256]{3,2,1,0:T(8,128)S(1)}, f32[2,16,16,256]{3,2,1,0:T(8,128)S(1)}) custom-call(s32[16]{0:T(128)S(1)} %multiply_add_fusion.slot_ref, s32[16]{0:T(128)S(1)} %reshape.342.present_ref, bf16[2,16,16,256]{3,2,1,0:T(8,128)(2,1)S(1)} %fusion.10.inputs_ref, bf16[32,3,16,256]{3,2,1,0:T(8,128)(2,1)S(1)} %bitcast.234, ...), custom_call_target="tpu_custom_call" | custom-call | tf_op jit(solution)/shard_map/forward_conv/pallas_call | solution.py:185
  71.4 1.0 copy-done.2
  73.1 0.7 copy-done.10
  74.3 1.2 fusion.4
  75.5 0.6 fusion.30
  76.6 9.3 %backward_conv.2 = (f32[2,16,16,256]{3,2,1,0:T(8,128)S(1)}, bf16[32,3,16,256]{3,2,1,0:T(8,128)(2,1)}) custom-call(s32[16]{0:T(128)S(1)} %multiply_add_fusion.slot_ref, s32[16]{0:T(128)S(1)} %reshape.342.present_ref, f32[2,16,16,256]{3,2,1,0:T(8,128)S(1)} %bitcast.239, f32[49,256]{1,0:T(8,128)S(1)} %get-tuple-element.66.kernel_ref), custom_call_target="tpu_custom_call" | custom-call | flops 7699999744 | bytes 25200000 | tf_op jit(solution)/shard_map/backward_conv/pallas_call | solution.py:311
  85.9 9.4 %all-to-all-start = ((bf16[16,2,3,16,256]{4,3,2,1,0:T(8,128)(2,1)}), bf16[16,2,3,16,256]{4,3,2,1,0:T(8,128)(2,1)S(1)}, u32[]{:S(2)}, u32[]{:S(2)}) async-start(bf16[16,2,3,16,256]{4,3,2,1,0:T(8,128)(2,1)} %bitcast.21), calls=%async_computation | async-start | bytes 1572864 | tf_op jit(solution)/shard_map/all_to_all | solution.py:420
  95.3 3.3 %fusion.11 = f32[1024,256]{0,1:T(8,128)} fusion(bf16[512,256]{1,0:T(8,128)(2,1)S(1)} %bitcast.260, f32[512,1024]{1,0:T(8,128)} %copy-done.6), kind=kOutput, calls=%fused_computation.25 | convolution fusion | flops 271056896 | bytes 3407872 | tf_op jit(solution)/shard_map/dot_general | solution.py:392
  98.7 1.8 convolution_bitcast_fusion
  100.5 1.1 fusion.21
  102.0 3.5 %tap_sums.3 = f32[49,256]{1,0:T(8,128)S(1)} custom-call(f32[2,22,24,256]{3,2,1,0:T(8,128)S(1)} %copy-done.3, f32[2,16,16,256]{3,2,1,0:T(8,128)S(1)} %bitcast.240), custom_call_target="tpu_custom_call" | custom-call | flops 5500000256 | bytes 18000000 | tf_op jit(solution)/shard_map/tap_sums/pallas_call | solution.py:243
  105.7 1.9 bitcast_add_fusion
  107.8 0.8 fusion.49
  108.5 1.9 collective-permute-start.5
  110.6 9.8 %collective-permute-done.13 = f32[50,256]{1,0:T(8,128)S(1)} collective-permute-done((f32[50,256]{1,0:T(8,128)S(1)}, f32[50,256]{1,0:T(8,128)S(1)}, u32[]{:S(2)}, u32[]{:S(2)}) %collective-permute-start.13) | collective-permute-done | bytes 51232 | tf_op jit(solution)/shard_map/ppermute | solution.py:414
  120.5 0.9 collective-permute-start.14
  121.5 0.8 copy.62
  122.3 2.4 %collective-permute-done.14 = f32[50,256]{1,0:T(8,128)S(1)} collective-permute-done((f32[50,256]{1,0:T(8,128)S(1)}, f32[50,256]{1,0:T(8,128)S(1)}, u32[]{:S(2)}, u32[]{:S(2)}) %collective-permute-start.14) | collective-permute-done | bytes 51232 | tf_op jit(solution)/shard_map/ppermute | solution.py:414
  124.7 1.8 collective-permute-start.15
  126.5 1.4 bitcast_add_fusion.1
  127.9 1.4 collective-permute-start.6
  129.3 1.0 collective-permute-done.15
  130.3 0.6 add_bitcast_fusion
  131.0 2.0 collective-permute-done.6
  133.0 0.7 fusion.53
  133.7 1.2 collect.2.base_ref
  135.1 1.8 convolution_bitcast_fusion.1
  137.2 1.1 fusion.9
  138.5 0.6 fusion.26
  140.1 3.5 %tap_sums.2 = f32[49,256]{1,0:T(8,128)S(1)} custom-call(f32[2,22,24,256]{3,2,1,0:T(8,128)S(1)} %get-tuple-element.24.padded_ref, f32[2,16,16,256]{3,2,1,0:T(8,128)S(1)} %bitcast.237), custom_call_target="tpu_custom_call" | custom-call | flops 5500000256 | bytes 18000000 | tf_op jit(solution)/shard_map/tap_sums/pallas_call | solution.py:243
  143.8 0.6 collective-permute-start
  144.5 1.3 collective-permute-start.7
  145.8 0.9 collective-permute-start.9
  146.7 4.1 %collective-permute-done.7 = bf16[1,16,2,1024]{3,1,2,0:T(8,128)(2,1)S(1)} collective-permute-done((bf16[1,16,2,1024]{3,1,2,0:T(8,128)(2,1)S(1)}, bf16[1,16,2,1024]{3,1,2,0:T(8,128)(2,1)S(1)}, u32[]{:S(2)}, u32[]{:S(2)}) %collective-permute-start.7) | collective-permute-done | bytes 65568 | tf_op jit(solution)/shard_map/ppermute | solution.py:406
  151.6 1.7 collective-permute-start.1
  153.3 8.4 %backward_conv.3 = (f32[2,16,16,256]{3,2,1,0:T(8,128)S(1)}, bf16[32,3,16,256]{3,2,1,0:T(8,128)(2,1)}) custom-call(s32[16]{0:T(128)S(1)} %multiply_add_fusion.slot_ref, s32[16]{0:T(128)S(1)} %reshape.342.present_ref, f32[2,16,16,256]{3,2,1,0:T(8,128)S(1)} %bitcast.238, f32[49,256]{1,0:T(8,128)S(1)} %get-tuple-element.67.kernel_ref), custom_call_target="tpu_custom_call" | custom-call | flops 7699999744 | bytes 25200000 | tf_op jit(solution)/shard_map/backward_conv/pallas_call | solution.py:311
  161.7 3.7 %all-to-all-start.1 = ((bf16[16,2,3,16,256]{4,3,2,1,0:T(8,128)(2,1)}), bf16[16,2,3,16,256]{4,3,2,1,0:T(8,128)(2,1)S(1)}, u32[]{:S(2)}, u32[]{:S(2)}) async-start(bf16[16,2,3,16,256]{4,3,2,1,0:T(8,128)(2,1)} %bitcast.26), calls=%async_computation.1 | async-start | bytes 1572864 | tf_op jit(solution)/shard_map/all_to_all | solution.py:420
  165.4 2.8 %collective-permute-start.11 = (f32[50,256]{1,0:T(8,128)S(1)}, f32[50,256]{1,0:T(8,128)S(1)}, u32[]{:S(2)}, u32[]{:S(2)}) collective-permute-start(f32[50,256]{1,0:T(8,128)S(1)} %add.146), channel_id=1, source_target_pairs={{0,8},{1,9},{2,10},{3,11},{4,12},{5,13},{6,14},{7,15},{8,0},{9,1},... | collective-permute-start | bytes 153608 | tf_op jit(solution)/shard_map/ppermute | solution.py:414
  168.3 1.0 bitcast_add_fusion.2
  169.3 1.6 collective-permute-start.2
  170.9 17.8 %collective-permute-done.11 = f32[50,256]{1,0:T(8,128)S(1)} collective-permute-done((f32[50,256]{1,0:T(8,128)S(1)}, f32[50,256]{1,0:T(8,128)S(1)}, u32[]{:S(2)}, u32[]{:S(2)}) %collective-permute-start.11) | collective-permute-done | bytes 51232 | tf_op jit(solution)/shard_map/ppermute | solution.py:414
  188.8 0.7 copy.83
  189.6 0.6 copy.125
  190.2 4.6 %collective-permute-done.3 = bf16[1,16,2,1024]{3,1,2,0:T(8,128)(2,1)S(1)} collective-permute-done((bf16[1,16,2,1024]{3,1,2,0:T(8,128)(2,1)S(1)}, bf16[1,16,2,1024]{3,1,2,0:T(8,128)(2,1)S(1)}, u32[]{:S(2)}, u32[]{:S(2)}) %collective-permute-start.3) | collective-permute-done | bytes 65568 | tf_op jit(solution)/shard_map/ppermute | solution.py:406
  194.8 0.8 copy.82
  195.6 0.8 copy.81
  196.3 1.2 collect.3
  197.5 0.7 convert_element_type.136
  (128 shorter events, 7.4 us)
Async XLA Ops:
  0.6 34.6 %copy-start.1 = (bf16[2,16,16,256]{3,2,1,0:T(8,128)(2,1)S(1)}, bf16[2,16,16,256]{3,2,1,0:T(8,128)(2,1)}, u32[]{:S(2)}) copy-start(bf16[2,16,16,256]{3,2,1,0:T(8,128)(2,1)} %inputs_ref.3) | copy-start | bytes 786436
  15.6 1.0 copy-start
  35.2 5.7 %copy-start.18 = (bf16[2,256,1024]{2,1,0:T(8,128)(2,1)S(1)}, bf16[2,256,1024]{2,1,0:T(8,128)(2,1)}, u32[]{:S(2)}) copy-start(bf16[2,256,1024]{2,1,0:T(8,128)(2,1)} %param.16) | copy-start | bytes 3145732
  40.9 1.8 copy-start.12
  40.9 2.8 %copy-start.25 = (bf16[2,1024,256]{2,1,0:T(8,128)(2,1)S(1)}, bf16[2,1024,256]{2,1,0:T(8,128)(2,1)}, u32[]{:S(2)}) copy-start(bf16[2,1024,256]{2,1,0:T(8,128)(2,1)} %param.17) | copy-start | bytes 3145732
  42.8 1.0 copy-start.9
  71.3 1.0 copy-start.2
  72.8 1.4 copy-start.21
  72.9 1.4 copy-start.26
  73.1 0.7 copy-start.10
  74.2 1.3 copy-start.6
  75.5 1.1 copy-start.20
  76.6 18.7 %copy-start.22 = (bf16[2,16,16,256]{3,2,1,0:T(8,128)(2,1)S(1)}, bf16[2,16,16,256]{3,2,1,0:T(8,128)(2,1)}, u32[]{:S(2)}) copy-start(bf16[2,16,16,256]{3,2,1,0:T(8,128)(2,1)} %param.18) | copy-start | bytes 786436
  85.9 47.8 %all-to-all-start = ((bf16[16,2,3,16,256]{4,3,2,1,0:T(8,128)(2,1)}), bf16[16,2,3,16,256]{4,3,2,1,0:T(8,128)(2,1)S(1)}, u32[]{:S(2)}, u32[]{:S(2)}) async-start(bf16[16,2,3,16,256]{4,3,2,1,0:T(8,128)(2,1)} %bitcast.21), calls=%async_computation | async-start | bytes 1572864 | tf_op jit(solution)/shard_map/all_to_all | solution.py:420
  95.2 3.3 %copy-start.11 = (bf16[2,16,16,256]{3,2,1,0:T(8,128)(2,1)S(1)}, bf16[2,16,16,256]{3,2,1,0:T(8,128)(2,1)}, u32[]{:S(2)}) copy-start(bf16[2,16,16,256]{3,2,1,0:T(8,128)(2,1)} %copy-done.10) | copy-start | bytes 786436
  98.7 1.9 copy-start.4
  98.7 3.3 %copy-start.3 = (f32[2,22,24,256]{3,2,1,0:T(8,128)S(1)}, f32[2,22,24,256]{3,2,1,0:T(8,128)}, u32[]{:S(2)}) copy-start(f32[2,22,24,256]{3,2,1,0:T(8,128)} %copy-done.2) | copy-start | bytes 3244036
  100.5 1.5 copy-start.5
  101.6 4.1 %collective-permute-start.4 = (bf16[8,16,2,1024]{3,1,0,2:T(8,128)(2,1)}, bf16[8,16,2,1024]{3,1,0,2:T(8,128)(2,1)}, u32[]{:S(2)}, u32[]{:S(2)}) collective-permute-start(bf16[8,16,2,1024]{3,1,0,2:T(8,128)(2,1)} %fusion.21), channel_id=1, source_target_pairs={{0,1},{1,0},{2,3},{3,2},{4,5},{5,4},{6,7},{7,6},{8,9},{9,8},{10,11... | collective-permute-start | bytes 1572872 | tf_op jit(solution)/shard_map/ppermute | solution.py:406
  105.5 4.9 %collective-permute-start.12 = (f32[50,256]{1,0:T(8,128)S(1)}, f32[50,256]{1,0:T(8,128)S(1)}, u32[]{:S(2)}, u32[]{:S(2)}) collective-permute-start(f32[50,256]{1,0:T(8,128)S(1)} %pad_maximum_fusion.4), channel_id=1, source_target_pairs={{0,1},{1,0},{2,3},{3,2},{4,5},{5,4},{6,7},{7,6},{8,9},{9,8},{10,11... | collective-permute-start | bytes 153608 | tf_op jit(solution)/shard_map/ppermute | solution.py:414
  107.6 13.8 %copy-start.23 = (bf16[2,16,16,256]{3,2,1,0:T(8,128)(2,1)S(1)}, bf16[2,16,16,256]{3,2,1,0:T(8,128)(2,1)}, u32[]{:S(2)}) copy-start(bf16[2,16,16,256]{3,2,1,0:T(8,128)(2,1)} %param.18) | copy-start | bytes 786436
  107.6 13.9 %copy-start.13 = (bf16[2,16,16,256]{3,2,1,0:T(8,128)(2,1)S(1)}, bf16[2,16,16,256]{3,2,1,0:T(8,128)(2,1)}, u32[]{:S(2)}) copy-start(bf16[2,16,16,256]{3,2,1,0:T(8,128)(2,1)} %copy-done.12) | copy-start | bytes 786436
  107.7 12.7 %copy-start.7 = (f32[4,1,16,2,1024]{4,2,1,0,3:T(8,128)}, f32[4,1,16,2,1024]{4,2,1,0,3:T(8,128)S(1)}, u32[]{:S(2)}) copy-start(f32[4,1,16,2,1024]{4,2,1,0,3:T(8,128)S(1)} %get-tuple-element.52) | copy-start | bytes 1572868
  107.7 13.6 %copy-start.8 = (f32[4,1,16,2,1024]{4,2,1,0,3:T(8,128)}, f32[4,1,16,2,1024]{4,2,1,0,3:T(8,128)S(1)}, u32[]{:S(2)}) copy-start(f32[4,1,16,2,1024]{4,2,1,0,3:T(8,128)S(1)} %get-tuple-element.53) | copy-start | bytes 1572868
  108.5 18.0 %collective-permute-start.5 = (bf16[4,16,2,1024]{3,1,2,0:T(8,128)(2,1)}, bf16[4,16,2,1024]{3,1,2,0:T(8,128)(2,1)}, u32[]{:S(2)}, u32[]{:S(2)}) collective-permute-start(bf16[4,16,2,1024]{3,1,2,0:T(8,128)(2,1)} %fusion.49), channel_id=1, source_target_pairs={{0,2},{1,3},{2,0},{3,1},{4,6},{5,7},{6,4},{7,5},{8,10},{9,11},{10,... | collective-permute-start | bytes 786440 | tf_op jit(solution)/shard_map/ppermute | solution.py:406
  110.4 10.0 %collective-permute-start.13 = (f32[50,256]{1,0:T(8,128)S(1)}, f32[50,256]{1,0:T(8,128)S(1)}, u32[]{:S(2)}, u32[]{:S(2)}) collective-permute-start(f32[50,256]{1,0:T(8,128)S(1)} %fusion.84), channel_id=1, source_target_pairs={{0,2},{1,3},{2,0},{3,1},{4,6},{5,7},{6,4},{7,5},{8,10},{9,11},{10,... | collective-permute-start | bytes 153608 | tf_op jit(solution)/shard_map/ppermute | solution.py:414
  120.5 4.2 %collective-permute-start.14 = (f32[50,256]{1,0:T(8,128)S(1)}, f32[50,256]{1,0:T(8,128)S(1)}, u32[]{:S(2)}, u32[]{:S(2)}) collective-permute-start(f32[50,256]{1,0:T(8,128)S(1)} %add.149), channel_id=1, source_target_pairs={{0,4},{1,5},{2,6},{3,7},{4,0},{5,1},{6,2},{7,3},{8,12},{9,13},{10,... | collective-permute-start | bytes 153608 | tf_op jit(solution)/shard_map/ppermute | solution.py:414
  124.7 5.6 %collective-permute-start.15 = (f32[50,256]{1,0:T(8,128)S(1)}, f32[50,256]{1,0:T(8,128)S(1)}, u32[]{:S(2)}, u32[]{:S(2)}) collective-permute-start(f32[50,256]{1,0:T(8,128)S(1)} %add.150), channel_id=1, source_target_pairs={{0,8},{1,9},{2,10},{3,11},{4,12},{5,13},{6,14},{7,15},{8,0},{9,1},... | collective-permute-start | bytes 153608 | tf_op jit(solution)/shard_map/ppermute | solution.py:414
  127.9 5.0 %collective-permute-start.6 = (bf16[2,16,2,1024]{3,1,2,0:T(8,128)(2,1)S(1)}, bf16[2,16,2,1024]{3,1,2,0:T(8,128)(2,1)S(1)}, u32[]{:S(2)}, u32[]{:S(2)}) collective-permute-start(bf16[2,16,2,1024]{3,1,2,0:T(8,128)(2,1)S(1)} %fusion.56), channel_id=1, source_target_pairs={{0,4},{1,5},{2,6},{3,7},{4,0},{5,1},{6,2},{7,3},{8,12},{9,13},{10,... | collective-permute-start | bytes 393224 | tf_op jit(solution)/shard_map/ppermute | solution.py:406
  134.9 2.0 %copy-start.27 = (bf16[2,1024,256]{2,1,0:T(8,128)(2,1)S(1)}, bf16[2,1024,256]{2,1,0:T(8,128)(2,1)}, u32[]{:S(2)}) copy-start(bf16[2,1024,256]{2,1,0:T(8,128)(2,1)} %param.17) | copy-start | bytes 3145732
  135.1 2.1 %copy-start.15 = (f32[512,1024]{1,0:T(8,128)S(1)}, f32[512,1024]{1,0:T(8,128)}, u32[]{:S(2)}) copy-start(f32[512,1024]{1,0:T(8,128)} %get-tuple-element.63) | copy-start | bytes 6291460
  137.2 1.2 copy-start.14
  137.2 1.4 copy-start.19
  138.3 1.0 copy-start.17
  143.6 1.0 copy-start.16
  143.6 2.2 %collective-permute-start.8 = (f32[50,256]{1,0:T(8,128)S(1)}, f32[50,256]{1,0:T(8,128)S(1)}, u32[]{:S(2)}, u32[]{:S(2)}) collective-permute-start(f32[50,256]{1,0:T(8,128)S(1)} %pad_maximum_fusion.3), channel_id=1, source_target_pairs={{0,1},{1,0},{2,3},{3,2},{4,5},{5,4},{6,7},{7,6},{8,9},{9,8},{10,11... | collective-permute-start | bytes 153608 | tf_op jit(solution)/shard_map/ppermute | solution.py:414
  143.8 7.4 %collective-permute-start = (bf16[8,16,2,1024]{3,1,0,2:T(8,128)(2,1)S(1)}, bf16[8,16,2,1024]{3,1,0,2:T(8,128)(2,1)S(1)}, u32[]{:S(2)}, u32[]{:S(2)}) collective-permute-start(bf16[8,16,2,1024]{3,1,0,2:T(8,128)(2,1)S(1)} %fusion.20), channel_id=1, source_target_pairs={{0,1},{1,0},{2,3},{3,2},{4,5},{5,4},{6,7},{7,6},{8,9},{9,8},{10,11... | collective-permute-start | bytes 1572872 | tf_op jit(solution)/shard_map/ppermute | solution.py:406
  144.5 6.3 %collective-permute-start.7 = (bf16[1,16,2,1024]{3,1,2,0:T(8,128)(2,1)S(1)}, bf16[1,16,2,1024]{3,1,2,0:T(8,128)(2,1)S(1)}, u32[]{:S(2)}, u32[]{:S(2)}) collective-permute-start(bf16[1,16,2,1024]{3,1,2,0:T(8,128)(2,1)S(1)} %fusion.65), channel_id=1, source_target_pairs={{0,8},{1,9},{2,10},{3,11},{4,12},{5,13},{6,14},{7,15},{8,0},{9,1},... | collective-permute-start | bytes 196616 | tf_op jit(solution)/shard_map/ppermute | solution.py:406
  145.8 5.0 %collective-permute-start.9 = (f32[50,256]{1,0:T(8,128)S(1)}, f32[50,256]{1,0:T(8,128)S(1)}, u32[]{:S(2)}, u32[]{:S(2)}) collective-permute-start(f32[50,256]{1,0:T(8,128)S(1)} %fusion.83), channel_id=1, source_target_pairs={{0,2},{1,3},{2,0},{3,1},{4,6},{5,7},{6,4},{7,5},{8,10},{9,11},{10,... | collective-permute-start | bytes 153608 | tf_op jit(solution)/shard_map/ppermute | solution.py:414
  150.9 14.5 %collective-permute-start.10 = (f32[50,256]{1,0:T(8,128)S(1)}, f32[50,256]{1,0:T(8,128)S(1)}, u32[]{:S(2)}, u32[]{:S(2)}) collective-permute-start(f32[50,256]{1,0:T(8,128)S(1)} %add.145), channel_id=1, source_target_pairs={{0,4},{1,5},{2,6},{3,7},{4,0},{5,1},{6,2},{7,3},{8,12},{9,13},{10,... | collective-permute-start | bytes 153608 | tf_op jit(solution)/shard_map/ppermute | solution.py:414
  151.6 16.7 %collective-permute-start.1 = (bf16[4,16,2,1024]{3,1,2,0:T(8,128)(2,1)S(1)}, bf16[4,16,2,1024]{3,1,2,0:T(8,128)(2,1)}, u32[]{:S(2)}, u32[]{:S(2)}) collective-permute-start(bf16[4,16,2,1024]{3,1,2,0:T(8,128)(2,1)S(1)} %fusion.48), channel_id=1, source_target_pairs={{0,2},{1,3},{2,0},{3,1},{4,6},{5,7},{6,4},{7,5},{8,10},{9,11},{10,... | collective-permute-start | bytes 786440 | tf_op jit(solution)/shard_map/ppermute | solution.py:406
  161.7 27.1 %copy-start.24 = (f32[1,50,256]{2,1,0:T(8,128)S(1)}, f32[1,50,256]{2,1,0:T(8,128)}, u32[]{:S(2)}) copy-start(f32[1,50,256]{2,1,0:T(8,128)} %add_bitcast_fusion) | copy-start | bytes 153604
  161.7 34.7 %all-to-all-start.1 = ((bf16[16,2,3,16,256]{4,3,2,1,0:T(8,128)(2,1)}), bf16[16,2,3,16,256]{4,3,2,1,0:T(8,128)(2,1)S(1)}, u32[]{:S(2)}, u32[]{:S(2)}) async-start(bf16[16,2,3,16,256]{4,3,2,1,0:T(8,128)(2,1)} %bitcast.26), calls=%async_computation.1 | async-start | bytes 1572864 | tf_op jit(solution)/shard_map/all_to_all | solution.py:420
  165.4 23.3 %collective-permute-start.11 = (f32[50,256]{1,0:T(8,128)S(1)}, f32[50,256]{1,0:T(8,128)S(1)}, u32[]{:S(2)}, u32[]{:S(2)}) collective-permute-start(f32[50,256]{1,0:T(8,128)S(1)} %add.146), channel_id=1, source_target_pairs={{0,8},{1,9},{2,10},{3,11},{4,12},{5,13},{6,14},{7,15},{8,0},{9,1},... | collective-permute-start | bytes 153608 | tf_op jit(solution)/shard_map/ppermute | solution.py:414
  169.3 20.1 %collective-permute-start.2 = (bf16[2,16,2,1024]{3,1,2,0:T(8,128)(2,1)S(1)}, bf16[2,16,2,1024]{3,1,2,0:T(8,128)(2,1)S(1)}, u32[]{:S(2)}, u32[]{:S(2)}) collective-permute-start(bf16[2,16,2,1024]{3,1,2,0:T(8,128)(2,1)S(1)} %fusion.55), channel_id=1, source_target_pairs={{0,4},{1,5},{2,6},{3,7},{4,0},{5,1},{6,2},{7,3},{8,12},{9,13},{10,... | collective-permute-start | bytes 393224 | tf_op jit(solution)/shard_map/ppermute | solution.py:406
  189.5 5.2 %collective-permute-start.3 = (bf16[1,16,2,1024]{3,1,2,0:T(8,128)(2,1)S(1)}, bf16[1,16,2,1024]{3,1,2,0:T(8,128)(2,1)S(1)}, u32[]{:S(2)}, u32[]{:S(2)}) collective-permute-start(bf16[1,16,2,1024]{3,1,2,0:T(8,128)(2,1)S(1)} %fusion.64), channel_id=1, source_target_pairs={{0,8},{1,9},{2,10},{3,11},{4,12},{5,13},{6,14},{7,15},{8,0},{9,1},... | collective-permute-start | bytes 196616 | tf_op jit(solution)/shard_map/ppermute | solution.py:406

commit v2 on v1

--- a/solution.py
+++ b/solution.py
@@ -490,14 +490,19 @@
         if layer_index > 0:
             outgoing, back_conv, slope = lax.optimization_barrier((outgoing, back_conv, slope))
             operand_set = (row_block, slope, rounded, hidden)
-        weight_terms[layer_index] = halve(pair_term(operand_set), steps)
-        kernel_term = tap_sums(kept, back_conv)
-        small_terms[layer_index] = double(
-            jnp.concatenate([kernel_term, gain_term[None]], axis=0), steps
-        )
-        gradient = collect(gradient, centre, exchange(outgoing, peers), wanted)
+        terms = pair_term(operand_set)
+        small_terms[layer_index] = jnp.concatenate(
+            [tap_sums(kept, back_conv), gain_term[None]], axis=0
+        )
+        if layer_index > 0:
+            returned = exchange(outgoing, peers)
+            returned, terms = lax.optimization_barrier((returned, terms))
+        else:
+            returned = direct_exchange(outgoing, peers, 1)
+        weight_terms[layer_index] = halve(terms, steps)
+        gradient = collect(gradient, centre, returned, wanted)
     weights_part = jnp.stack(weight_terms, axis=2)
-    small = jnp.stack(small_terms)
+    small = double(jnp.stack(small_terms), steps)
     kernel_sum, gain_sum = small[:, :-1], small[:, -1]
     grad_tiles = gradient.astype(jnp.bfloat16)
     return (

time: 199 us -> 195 us (0.980)
  waiting for transfers between devices: 41.8 us -> 26.1 us
  Pallas kernels: 86 us -> 97.6 us
  starting transfers between devices: 29.1 us -> 33.5 us
  other arithmetic: 14 us -> 10.2 us
    ppermute x8 -> x4, waiting for transfers between devices: 31.1 us -> 6.54 us  [double(): values = values + lax.ppermute(values, 'tile', partners)]
    pallas_call x3 -> x4, Pallas kernels: 48.2 us -> 63.9 us  [direct_exchange(): pl.pallas_call(functools.partial(exchange_kernel, peers), out_shape=jax.S...]
    ppermute x8, starting transfers between devices: 8.84 us -> 16.6 us  [halve(): values = kept + lax.ppermute(sent, 'tile', partners).astype(jnp.float32)]
    all_to_all x2 -> x1, waiting for transfers between devices: 0.01 us -> 7.11 us  [exchange(): lax.all_to_all(arranged, 'tile', split_axis=0, concat_axis=0, tiled=True)]
    add x4, other arithmetic: 4.58 us -> 0.72 us  [halve(): values = kept + lax.ppermute(sent, 'tile', partners).astype(jnp.float32)]
    dot_general x2, matrix products: 5.08 us -> 1.3 us  [pair_term(): lax.dot_general(rounded, hidden, dims_rows, preferred_element_type=jnp.fl...]
    all_to_all x2 -> x1, starting transfers between devices: 13.1 us -> 9.36 us  [exchange(): lax.all_to_all(arranged, 'tile', split_axis=0, concat_axis=0, tiled=True)]
    pallas_call x2, Pallas kernels: 17.6 us -> 14.5 us  [backward_conv(): pl.pallas_call(backward_kernel, out_shape=(jax.ShapeDtypeStruct(back_conv...]
  transfers between devices with their start and end apart: 18 -> 13, of which waited for: 7 -> 8; matrix products, arithmetic and copies ran while one was open for 9% -> 6% of each run, Pallas kernels for 6% -> 10%
where the time goes in v2:
time: 195 us; the launch traced here: 194 us
  Pallas kernels  97.6 us (50%)
  starting transfers between devices  33.5 us (17%)
  waiting for transfers between devices  26.1 us (13%)
  local copies, waits for them, and re-layouts  13.2 us (7%)
  matrix products  12.3 us (6%)
  other arithmetic  10.2 us (5%)
    pallas_call x4, Pallas kernels, direct_exchange(): pl.pallas_call(functools.partial(exchange_kernel, peers), out_shape=jax.S...  63.9 us
    ppermute x8, starting transfers between devices, halve(): values = kept + lax.ppermute(sent, 'tile', partners).astype(jnp.float32)  16.6 us
    pallas_call x2, Pallas kernels, backward_conv(): pl.pallas_call(backward_kernel, out_shape=(jax.ShapeDtypeStruct(back_conv...  14.5 us
    ppermute x8, waiting for transfers between devices, halve(): values = kept + lax.ppermute(sent, 'tile', partners).astype(jnp.float32)  12.4 us
    all_to_all x1, starting transfers between devices, exchange(): lax.all_to_all(arranged, 'tile', split_axis=0, concat_axis=0, tiled=True)  9.36 us
    unnamed x51, local copies, waits for them, and re-layouts  7.81 us
    pallas_call x2, Pallas kernels, forward_conv(): pl.pallas_call(forward_kernel, out_shape=(jax.ShapeDtypeStruct((tiles, ex...  7.8 us
    ppermute x4, starting transfers between devices, double(): values = values + lax.ppermute(values, 'tile', partners)  7.55 us
  transfers between devices with their start and end apart: 13, of which 8 were waited for; matrix products, arithmetic and copies ran while one was open for 6% of the time, Pallas kernels for 10%

profile of v2, /device:TPU:0, one launch (start us, length us, event | category | flops | bytes accessed | tf_op | source)
XLA Modules:
  0.0 194.2 jit_solution(17314653647083574945)
XLA Ops:
  0.6 0.8 reshape.333.present_ref
  1.4 0.5 broadcast.272
  2.0 1.3 reduce.7
  3.6 0.7 add_add_fusion
  4.4 0.8 fusion.68
  5.3 9.1 %exchange_requests.1 = s32[16,8,128]{2,1,0:T(8,128)S(1)} custom-call(s32[16,8,128]{2,1,0:T(8,128)S(1)} %pad.4.source_ref), custom_call_target="tpu_custom_call" | custom-call | tf_op jit(solution)/shard_map/exchange_requests/pallas_call | solution.py:81
  14.5 1.1 fusion.67
  15.6 0.9 copy-done
  16.5 1.1 serve.2
  17.6 17.6 %exchange_strips.3 = bf16[16,2,3,16,256]{4,3,2,1,0:T(8,128)(2,1)S(1)} custom-call(bf16[16,2,3,16,256]{4,3,2,1,0:T(8,128)(2,1)S(1)} %bitcast.249), custom_call_target="tpu_custom_call" | custom-call | tf_op jit(solution)/shard_map/exchange_strips/pallas_call | solution.py:81
  35.2 3.9 %forward_conv.2 = (f32[2,22,24,256]{3,2,1,0:T(8,128)S(1)}, f32[2,16,16,256]{3,2,1,0:T(8,128)S(1)}) custom-call(s32[16]{0:T(128)S(1)} %multiply_add_fusion.slot_ref, s32[16]{0:T(128)S(1)} %reshape.333.present_ref, bf16[2,16,16,256]{3,2,1,0:T(8,128)(2,1)S(1)} %copy-done.1, bf16[32,3,16,256]{3,2,1,0:T(8,128)(2,1)S(1)} %bitcast.247, ...), custom_call_target="tpu_custom_call" | custom-call | tf_op jit(solution)/shard_map/forward_conv/pallas_call | solution.py:185
  39.6 1.1 multiply_convert_fusion.4
  40.6 3.0 %multiply_convert_fusion.1 = (bf16[512,1024]{1,0:T(8,128)(2,1)S(1)}, f32[512,1024]{1,0:T(8,128)}) fusion(bf16[512,256]{1,0:T(8,128)(2,1)S(1)} %bitcast.267, bf16[2,256,1024]{2,1,0:T(8,128)(2,1)} %param.16), kind=kOutput, calls=%fused_computation.17 | convolution fusion | flops 271056896 | bytes 3932160 | tf_op jit(solution)/shard_map/dot_general | solution.py:449
  43.6 0.4 fusion.10.inputs_ref
  44.1 1.1 serve.3
  45.2 21.6 %exchange_strips.4 = bf16[16,2,3,16,256]{4,3,2,1,0:T(8,128)(2,1)S(1)} custom-call(bf16[16,2,3,16,256]{4,3,2,1,0:T(8,128)(2,1)S(1)} %bitcast.250), custom_call_target="tpu_custom_call" | custom-call | tf_op jit(solution)/shard_map/exchange_strips/pallas_call | solution.py:81
  66.7 3.9 %forward_conv.3 = (f32[2,22,24,256]{3,2,1,0:T(8,128)S(1)}, f32[2,16,16,256]{3,2,1,0:T(8,128)S(1)}) custom-call(s32[16]{0:T(128)S(1)} %multiply_add_fusion.slot_ref, s32[16]{0:T(128)S(1)} %reshape.333.present_ref, bf16[2,16,16,256]{3,2,1,0:T(8,128)(2,1)S(1)} %fusion.10.inputs_ref, bf16[32,3,16,256]{3,2,1,0:T(8,128)(2,1)S(1)} %bitcast.248, ...), custom_call_target="tpu_custom_call" | custom-call | tf_op jit(solution)/shard_map/forward_conv/pallas_call | solution.py:185
  70.7 1.0 copy-done.2
  72.4 1.7 fusion.30
  74.1 1.2 fusion.4
  75.4 0.7 copy-done.14
  76.1 0.6 fusion.27
  77.0 7.7 %backward_conv.2 = (f32[2,16,16,256]{3,2,1,0:T(8,128)S(1)}, bf16[32,3,16,256]{3,2,1,0:T(8,128)(2,1)}) custom-call(s32[16]{0:T(128)S(1)} %multiply_add_fusion.slot_ref, s32[16]{0:T(128)S(1)} %reshape.333.present_ref, f32[2,16,16,256]{3,2,1,0:T(8,128)S(1)} %bitcast.252, f32[49,256]{1,0:T(8,128)S(1)} %get-tuple-element.70.kernel_ref), custom_call_target="tpu_custom_call" | custom-call | flops 7699999744 | bytes 25200000 | tf_op jit(solution)/shard_map/backward_conv/pallas_call | solution.py:311
  84.7 9.4 %all-to-all-start = ((bf16[16,2,3,16,256]{4,3,2,1,0:T(8,128)(2,1)}), bf16[16,2,3,16,256]{4,3,2,1,0:T(8,128)(2,1)S(1)}, u32[]{:S(2)}, u32[]{:S(2)}) async-start(bf16[16,2,3,16,256]{4,3,2,1,0:T(8,128)(2,1)} %bitcast.21), calls=%async_computation | async-start | bytes 1572864 | tf_op jit(solution)/shard_map/all_to_all | solution.py:420
  94.0 1.0 convert_element_type.127.base_ref
  95.1 1.8 copy.64
  97.0 1.2 copy-done.3
  98.2 3.5 %tap_sums.3 = f32[49,256]{1,0:T(8,128)S(1)} custom-call(f32[2,22,24,256]{3,2,1,0:T(8,128)S(1)} %copy-done.3, f32[2,16,16,256]{3,2,1,0:T(8,128)S(1)} %bitcast.253), custom_call_target="tpu_custom_call" | custom-call | flops 5500000256 | bytes 18000000 | tf_op jit(solution)/shard_map/tap_sums/pallas_call | solution.py:243
  101.7 0.6 maximum_bitcast_fusion.1
  102.3 0.5 convolution_bitcast_fusion.3
  102.8 0.5 copy-done.6
  103.3 0.9 convolution_bitcast_fusion.2
  104.2 1.5 pad_maximum_fusion
  105.6 7.1 %all-to-all-done = bf16[16,2,3,16,256]{4,3,2,1,0:T(8,128)(2,1)S(1)} async-done(((bf16[16,2,3,16,256]{4,3,2,1,0:T(8,128)(2,1)}), bf16[16,2,3,16,256]{4,3,2,1,0:T(8,128)(2,1)S(1)}, u32[]{:S(2)}, u32[]{:S(2)}) %all-to-all-start) | async-done | bytes 786464 | tf_op jit(solution)/shard_map/all_to_all | solution.py:420
  112.7 1.2 collect.2.base_ref
  114.1 2.6 %fusion.9 = bf16[512,1024]{1,0:T(8,128)(2,1)S(1)} fusion(f32[512,1024]{1,0:T(8,128)} %get-tuple-element.67, bf16[512,256]{1,0:T(8,128)(2,1)S(1)} %bitcast.272, bf16[2,1024,256]{2,1,0:T(8,128)(2,1)} %param.17), kind=kOutput, calls=%fused_computation.11 | convolution fusion | flops 273678336 | bytes 3932160 | tf_op jit(solution)/shard_map/dot_general | solution.py:472
  116.8 0.6 fusion.23
  117.7 6.8 %backward_conv.3 = (f32[2,16,16,256]{3,2,1,0:T(8,128)S(1)}, bf16[32,3,16,256]{3,2,1,0:T(8,128)(2,1)S(1)}) custom-call(s32[16]{0:T(128)S(1)} %multiply_add_fusion.slot_ref, s32[16]{0:T(128)S(1)} %reshape.333.present_ref, f32[2,16,16,256]{3,2,1,0:T(8,128)S(1)} %bitcast.254, f32[49,256]{1,0:T(8,128)S(1)} %get-tuple-element.71.kernel_ref), custom_call_target="tpu_custom_call" | custom-call | flops 7699999744 | bytes 25200000 | tf_op jit(solution)/shard_map/backward_conv/pallas_call | solution.py:311
  124.5 3.5 %tap_sums.2 = f32[49,256]{1,0:T(8,128)S(1)} custom-call(f32[2,22,24,256]{3,2,1,0:T(8,128)S(1)} %get-tuple-element.28.padded_ref, f32[2,16,16,256]{3,2,1,0:T(8,128)S(1)} %bitcast.255), custom_call_target="tpu_custom_call" | custom-call | flops 5500000256 | bytes 18000000 | tf_op jit(solution)/shard_map/tap_sums/pallas_call | solution.py:243
  128.0 0.3 collective-permute-start.8
  128.3 0.4 convolution_bitcast_fusion
  128.8 0.6 collective-permute-done.8
  129.4 1.6 collective-permute-start.9
  131.0 0.5 convolution_bitcast_fusion.1
  131.5 3.3 %collective-permute-done.9 = f32[2,50,256]{2,1,0:T(8,128)S(1)} collective-permute-done((f32[2,50,256]{2,1,0:T(8,128)S(1)}, f32[2,50,256]{2,1,0:T(8,128)S(1)}, u32[]{:S(2)}, u32[]{:S(2)}) %collective-permute-start.9) | collective-permute-done | bytes 102432 | tf_op jit(solution)/shard_map/ppermute | solution.py:414
  134.8 2.7 %collective-permute-start.10 = (f32[2,50,256]{2,1,0:T(8,128)S(1)}, f32[2,50,256]{2,1,0:T(8,128)S(1)}, u32[]{:S(2)}, u32[]{:S(2)}) collective-permute-start(f32[2,50,256]{2,1,0:T(8,128)S(1)} %fusion.81), channel_id=1, source_target_pairs={{0,4},{1,5},{2,6},{3,7},{4,0},{5,1},{6,2},{7,3},{8,12},{9,13},{10,... | collective-permute-start | bytes 307208 | tf_op jit(solution)/shard_map/ppermute | solution.py:414
  137.8 2.6 %collective-permute-done.10 = f32[2,50,256]{2,1,0:T(8,128)S(1)} collective-permute-done((f32[2,50,256]{2,1,0:T(8,128)S(1)}, f32[2,50,256]{2,1,0:T(8,128)S(1)}, u32[]{:S(2)}, u32[]{:S(2)}) %collective-permute-start.10) | collective-permute-done | bytes 102432 | tf_op jit(solution)/shard_map/ppermute | solution.py:414
  140.4 2.9 %collective-permute-start.11 = (f32[2,50,256]{2,1,0:T(8,128)S(1)}, f32[2,50,256]{2,1,0:T(8,128)S(1)}, u32[]{:S(2)}, u32[]{:S(2)}) collective-permute-start(f32[2,50,256]{2,1,0:T(8,128)S(1)} %add.134), channel_id=1, source_target_pairs={{0,8},{1,9},{2,10},{3,11},{4,12},{5,13},{6,14},{7,15},{8,0},{9,1},... | collective-permute-start | bytes 307208 | tf_op jit(solution)/shard_map/ppermute | solution.py:414
  143.5 15.7 %exchange_strips.5 = bf16[16,2,3,16,256]{4,3,2,1,0:T(8,128)(2,1)S(1)} custom-call(bf16[16,2,3,16,256]{4,3,2,1,0:T(8,128)(2,1)S(1)} %bitcast.251), custom_call_target="tpu_custom_call" | custom-call | tf_op jit(solution)/shard_map/exchange_strips/pallas_call | solution.py:81
  159.2 1.2 collect.3
  160.4 0.7 convert_element_type.137
  161.2 0.7 copy.84
  161.9 0.6 copy.121
  162.9 2.4 %collective-permute-start.1 = (bf16[4,16,2,1024]{3,1,2,0:T(8,128)(2,1)S(1)}, bf16[4,16,2,1024]{3,1,2,0:T(8,128)(2,1)S(1)}, u32[]{:S(2)}, u32[]{:S(2)}) collective-permute-start(bf16[4,16,2,1024]{3,1,2,0:T(8,128)(2,1)S(1)} %fusion.45), channel_id=1, source_target_pairs={{0,2},{1,3},{2,0},{3,1},{4,6},{5,7},{6,4},{7,5},{8,10},{9,11},{10,... | collective-permute-start | bytes 786440 | tf_op jit(solution)/shard_map/ppermute | solution.py:406
  165.9 6.5 %collective-permute-done.1 = bf16[4,16,2,1024]{3,1,2,0:T(8,128)(2,1)S(1)} collective-permute-done((bf16[4,16,2,1024]{3,1,2,0:T(8,128)(2,1)S(1)}, bf16[4,16,2,1024]{3,1,2,0:T(8,128)(2,1)S(1)}, u32[]{:S(2)}, u32[]{:S(2)}) %collective-permute-start.1) | collective-permute-done | bytes 262176 | tf_op jit(solution)/shard_map/ppermute | solution.py:406
  172.5 5.0 %collective-permute-start.2 = (bf16[2,16,2,1024]{3,1,2,0:T(8,128)(2,1)S(1)}, bf16[2,16,2,1024]{3,1,2,0:T(8,128)(2,1)S(1)}, u32[]{:S(2)}, u32[]{:S(2)}) collective-permute-start(bf16[2,16,2,1024]{3,1,2,0:T(8,128)(2,1)S(1)} %fusion.51), channel_id=1, source_target_pairs={{0,4},{1,5},{2,6},{3,7},{4,0},{5,1},{6,2},{7,3},{8,12},{9,13},{10,... | collective-permute-start | bytes 393224 | tf_op jit(solution)/shard_map/ppermute | solution.py:406
  177.5 0.5 collective-permute-done.5
  178.1 4.9 %collective-permute-start.6 = (bf16[2,16,2,1024]{3,1,2,0:T(8,128)(2,1)S(1)}, bf16[2,16,2,1024]{3,1,2,0:T(8,128)(2,1)S(1)}, u32[]{:S(2)}, u32[]{:S(2)}) collective-permute-start(bf16[2,16,2,1024]{3,1,2,0:T(8,128)(2,1)S(1)} %fusion.52), channel_id=1, source_target_pairs={{0,4},{1,5},{2,6},{3,7},{4,0},{5,1},{6,2},{7,3},{8,12},{9,13},{10,... | collective-permute-start | bytes 393224 | tf_op jit(solution)/shard_map/ppermute | solution.py:406
  183.0 2.1 %collective-permute-start.3 = (bf16[1,16,2,1024]{3,1,2,0:T(8,128)(2,1)S(1)}, bf16[1,16,2,1024]{3,1,2,0:T(8,128)(2,1)S(1)}, u32[]{:S(2)}, u32[]{:S(2)}) collective-permute-start(bf16[1,16,2,1024]{3,1,2,0:T(8,128)(2,1)S(1)} %fusion.60), channel_id=1, source_target_pairs={{0,8},{1,9},{2,10},{3,11},{4,12},{5,13},{6,14},{7,15},{8,0},{9,1},... | collective-permute-start | bytes 196616 | tf_op jit(solution)/shard_map/ppermute | solution.py:406
  185.1 2.2 %collective-permute-done.6 = bf16[2,16,2,1024]{3,1,2,0:T(8,128)(2,1)S(1)} collective-permute-done((bf16[2,16,2,1024]{3,1,2,0:T(8,128)(2,1)S(1)}, bf16[2,16,2,1024]{3,1,2,0:T(8,128)(2,1)S(1)}, u32[]{:S(2)}, u32[]{:S(2)}) %collective-permute-start.6) | collective-permute-done | bytes 131104 | tf_op jit(solution)/shard_map/ppermute | solution.py:406
  187.4 1.9 collective-permute-start.7
  189.3 3.3 %collective-permute-done.7 = bf16[1,16,2,1024]{3,1,2,0:T(8,128)(2,1)S(1)} collective-permute-done((bf16[1,16,2,1024]{3,1,2,0:T(8,128)(2,1)S(1)}, bf16[1,16,2,1024]{3,1,2,0:T(8,128)(2,1)S(1)}, u32[]{:S(2)}, u32[]{:S(2)}) %collective-permute-start.7) | collective-permute-done | bytes 65568 | tf_op jit(solution)/shard_map/ppermute | solution.py:406
  192.7 0.8 copy.83
  193.4 0.8 copy.82
  (106 shorter events, 4.6 us)
Async XLA Ops:
  0.6 34.6 %copy-start.1 = (bf16[2,16,16,256]{3,2,1,0:T(8,128)(2,1)S(1)}, bf16[2,16,16,256]{3,2,1,0:T(8,128)(2,1)}, u32[]{:S(2)}) copy-start(bf16[2,16,16,256]{3,2,1,0:T(8,128)(2,1)} %inputs_ref.3) | copy-start | bytes 786436
  15.6 1.0 copy-start
  40.6 31.7 %copy-start.11 = (bf16[2,16,16,256]{3,2,1,0:T(8,128)(2,1)}, bf16[2,16,16,256]{3,2,1,0:T(8,128)(2,1)S(1)}, u32[]{:S(2)}) copy-start(bf16[2,16,16,256]{3,2,1,0:T(8,128)(2,1)S(1)} %get-tuple-element.54) | copy-start | bytes 786436
  40.6 3.0 %copy-start.21 = (bf16[2,1024,256]{2,1,0:T(8,128)(2,1)S(1)}, bf16[2,1024,256]{2,1,0:T(8,128)(2,1)}, u32[]{:S(2)}) copy-start(bf16[2,1024,256]{2,1,0:T(8,128)(2,1)} %param.17) | copy-start | bytes 3145732
  43.6 23.1 %copy-start.7 = (bf16[512,1024]{1,0:T(8,128)(2,1)}, bf16[512,1024]{1,0:T(8,128)(2,1)S(1)}, u32[]{:S(2)}) copy-start(bf16[512,1024]{1,0:T(8,128)(2,1)S(1)} %get-tuple-element.66) | copy-start | bytes 3145732
  70.6 1.0 copy-start.2
  72.1 2.0 %copy-start.18 = (bf16[2,16,16,256]{3,2,1,0:T(8,128)(2,1)S(1)}, bf16[2,16,16,256]{3,2,1,0:T(8,128)(2,1)}, u32[]{:S(2)}) copy-start(bf16[2,16,16,256]{3,2,1,0:T(8,128)(2,1)} %param.18) | copy-start | bytes 786436
  72.1 2.0 %copy-start.22 = (bf16[2,1024,256]{2,1,0:T(8,128)(2,1)S(1)}, bf16[2,1024,256]{2,1,0:T(8,128)(2,1)}, u32[]{:S(2)}) copy-start(bf16[2,1024,256]{2,1,0:T(8,128)(2,1)} %param.17) | copy-start | bytes 3145732
  72.4 2.9 %copy-start.9 = (bf16[2,16,16,256]{3,2,1,0:T(8,128)(2,1)}, bf16[2,16,16,256]{3,2,1,0:T(8,128)(2,1)S(1)}, u32[]{:S(2)}) copy-start(bf16[2,16,16,256]{3,2,1,0:T(8,128)(2,1)S(1)} %get-tuple-element.52) | copy-start | bytes 786436
  74.1 1.3 copy-start.5
  74.1 2.0 %copy-start.14 = (bf16[2,256,1024]{2,1,0:T(8,128)(2,1)S(1)}, bf16[2,256,1024]{2,1,0:T(8,128)(2,1)}, u32[]{:S(2)}) copy-start(bf16[2,256,1024]{2,1,0:T(8,128)(2,1)} %param.16) | copy-start | bytes 3145732
  75.4 1.6 copy-start.16
  84.7 28.1 %all-to-all-start = ((bf16[16,2,3,16,256]{4,3,2,1,0:T(8,128)(2,1)}), bf16[16,2,3,16,256]{4,3,2,1,0:T(8,128)(2,1)S(1)}, u32[]{:S(2)}, u32[]{:S(2)}) async-start(bf16[16,2,3,16,256]{4,3,2,1,0:T(8,128)(2,1)} %bitcast.21), calls=%async_computation | async-start | bytes 1572864 | tf_op jit(solution)/shard_map/all_to_all | solution.py:420
  97.0 1.2 copy-start.3
  98.2 4.1 %copy-start.10 = (bf16[2,16,16,256]{3,2,1,0:T(8,128)(2,1)S(1)}, bf16[2,16,16,256]{3,2,1,0:T(8,128)(2,1)}, u32[]{:S(2)}) copy-start(bf16[2,16,16,256]{3,2,1,0:T(8,128)(2,1)} %copy-done.9) | copy-start | bytes 786436
  98.2 4.1 %copy-start.17 = (bf16[512,1024]{1,0:T(8,128)(2,1)S(1)}, bf16[512,1024]{1,0:T(8,128)(2,1)}, u32[]{:S(2)}) copy-start(bf16[512,1024]{1,0:T(8,128)(2,1)} %copy-done.16) | copy-start | bytes 3145732
  101.7 1.6 copy-start.6
  101.7 1.6 copy-start.19
  114.1 2.7 %copy-start.12 = (f32[2,16,16,256]{3,2,1,0:T(8,128)S(1)}, f32[2,16,16,256]{3,2,1,0:T(8,128)}, u32[]{:S(2)}) copy-start(f32[2,16,16,256]{3,2,1,0:T(8,128)} %get-tuple-element.55) | copy-start | bytes 1572868
  114.1 2.7 %copy-start.15 = (bf16[2,256,1024]{2,1,0:T(8,128)(2,1)S(1)}, bf16[2,256,1024]{2,1,0:T(8,128)(2,1)}, u32[]{:S(2)}) copy-start(bf16[2,256,1024]{2,1,0:T(8,128)(2,1)} %param.16) | copy-start | bytes 3145732
  124.5 3.5 %copy-start.20 = (f32[1,50,256]{2,1,0:T(8,128)S(1)}, f32[1,50,256]{2,1,0:T(8,128)}, u32[]{:S(2)}) copy-start(f32[1,50,256]{2,1,0:T(8,128)} %maximum_bitcast_fusion.1) | copy-start | bytes 153604
  124.5 3.9 %copy-start.8 = (bf16[512,1024]{1,0:T(8,128)(2,1)S(1)}, bf16[512,1024]{1,0:T(8,128)(2,1)}, u32[]{:S(2)}) copy-start(bf16[512,1024]{1,0:T(8,128)(2,1)} %copy-done.7) | copy-start | bytes 3145732
  128.0 3.1 %copy-start.13 = (bf16[256,512]{1,0:T(8,128)(2,1)S(1)}, bf16[256,512]{1,0:T(8,128)(2,1)}, u32[]{:S(2)}) copy-start(bf16[256,512]{1,0:T(8,128)(2,1)} %copy.64) | copy-start | bytes 786436
  128.0 1.4 collective-permute-start.8
  129.4 5.4 %collective-permute-start.9 = (f32[2,50,256]{2,1,0:T(8,128)S(1)}, f32[2,50,256]{2,1,0:T(8,128)S(1)}, u32[]{:S(2)}, u32[]{:S(2)}) collective-permute-start(f32[2,50,256]{2,1,0:T(8,128)S(1)} %fusion.64), channel_id=1, source_target_pairs={{0,2},{1,3},{2,0},{3,1},{4,6},{5,7},{6,4},{7,5},{8,10},{9,11},{10,... | collective-permute-start | bytes 307208 | tf_op jit(solution)/shard_map/ppermute | solution.py:414
  131.5 11.9 %copy-start.4 = (f32[256,2,1024]{2,0,1:T(8,128)S(1)}, f32[256,2,1024]{2,0,1:T(8,128)}, u32[]{:S(2)}) copy-start(f32[256,2,1024]{2,0,1:T(8,128)} %pad_maximum_fusion) | copy-start | bytes 6291460
  134.8 5.6 %collective-permute-start.10 = (f32[2,50,256]{2,1,0:T(8,128)S(1)}, f32[2,50,256]{2,1,0:T(8,128)S(1)}, u32[]{:S(2)}, u32[]{:S(2)}) collective-permute-start(f32[2,50,256]{2,1,0:T(8,128)S(1)} %fusion.81), channel_id=1, source_target_pairs={{0,4},{1,5},{2,6},{3,7},{4,0},{5,1},{6,2},{7,3},{8,12},{9,13},{10,... | collective-permute-start | bytes 307208 | tf_op jit(solution)/shard_map/ppermute | solution.py:414
  137.7 24.7 %collective-permute-start = (bf16[8,16,2,1024]{3,1,0,2:T(8,128)(2,1)S(1)}, bf16[8,16,2,1024]{3,1,0,2:T(8,128)(2,1)S(1)}, u32[]{:S(2)}, u32[]{:S(2)}) collective-permute-start(bf16[8,16,2,1024]{3,1,0,2:T(8,128)(2,1)S(1)} %fusion.17), channel_id=1, source_target_pairs={{0,1},{1,0},{2,3},{3,2},{4,5},{5,4},{6,7},{7,6},{8,9},{9,8},{10,11... | collective-permute-start | bytes 1572872 | tf_op jit(solution)/shard_map/ppermute | solution.py:406
  140.4 20.7 %collective-permute-start.11 = (f32[2,50,256]{2,1,0:T(8,128)S(1)}, f32[2,50,256]{2,1,0:T(8,128)S(1)}, u32[]{:S(2)}, u32[]{:S(2)}) collective-permute-start(f32[2,50,256]{2,1,0:T(8,128)S(1)} %add.134), channel_id=1, source_target_pairs={{0,8},{1,9},{2,10},{3,11},{4,12},{5,13},{6,14},{7,15},{8,0},{9,1},... | collective-permute-start | bytes 307208 | tf_op jit(solution)/shard_map/ppermute | solution.py:414
  143.5 21.9 %collective-permute-start.4 = (bf16[8,16,2,1024]{3,1,0,2:T(8,128)(2,1)S(1)}, bf16[8,16,2,1024]{3,1,0,2:T(8,128)(2,1)S(1)}, u32[]{:S(2)}, u32[]{:S(2)}) collective-permute-start(bf16[8,16,2,1024]{3,1,0,2:T(8,128)(2,1)S(1)} %fusion.18), channel_id=1, source_target_pairs={{0,1},{1,0},{2,3},{3,2},{4,5},{5,4},{6,7},{7,6},{8,9},{9,8},{10,11... | collective-permute-start | bytes 1572872 | tf_op jit(solution)/shard_map/ppermute | solution.py:406
  162.9 9.4 %collective-permute-start.1 = (bf16[4,16,2,1024]{3,1,2,0:T(8,128)(2,1)S(1)}, bf16[4,16,2,1024]{3,1,2,0:T(8,128)(2,1)S(1)}, u32[]{:S(2)}, u32[]{:S(2)}) collective-permute-start(bf16[4,16,2,1024]{3,1,2,0:T(8,128)(2,1)S(1)} %fusion.45), channel_id=1, source_target_pairs={{0,2},{1,3},{2,0},{3,1},{4,6},{5,7},{6,4},{7,5},{8,10},{9,11},{10,... | collective-permute-start | bytes 786440 | tf_op jit(solution)/shard_map/ppermute | solution.py:406
  165.8 12.2 %collective-permute-start.5 = (bf16[4,16,2,1024]{3,1,2,0:T(8,128)(2,1)S(1)}, bf16[4,16,2,1024]{3,1,2,0:T(8,128)(2,1)S(1)}, u32[]{:S(2)}, u32[]{:S(2)}) collective-permute-start(bf16[4,16,2,1024]{3,1,2,0:T(8,128)(2,1)S(1)} %fusion.46), channel_id=1, source_target_pairs={{0,2},{1,3},{2,0},{3,1},{4,6},{5,7},{6,4},{7,5},{8,10},{9,11},{10,... | collective-permute-start | bytes 786440 | tf_op jit(solution)/shard_map/ppermute | solution.py:406
  172.5 10.5 %collective-permute-start.2 = (bf16[2,16,2,1024]{3,1,2,0:T(8,128)(2,1)S(1)}, bf16[2,16,2,1024]{3,1,2,0:T(8,128)(2,1)S(1)}, u32[]{:S(2)}, u32[]{:S(2)}) collective-permute-start(bf16[2,16,2,1024]{3,1,2,0:T(8,128)(2,1)S(1)} %fusion.51), channel_id=1, source_target_pairs={{0,4},{1,5},{2,6},{3,7},{4,0},{5,1},{6,2},{7,3},{8,12},{9,13},{10,... | collective-permute-start | bytes 393224 | tf_op jit(solution)/shard_map/ppermute | solution.py:406
  178.1 9.2 %collective-permute-start.6 = (bf16[2,16,2,1024]{3,1,2,0:T(8,128)(2,1)S(1)}, bf16[2,16,2,1024]{3,1,2,0:T(8,128)(2,1)S(1)}, u32[]{:S(2)}, u32[]{:S(2)}) collective-permute-start(bf16[2,16,2,1024]{3,1,2,0:T(8,128)(2,1)S(1)} %fusion.52), channel_id=1, source_target_pairs={{0,4},{1,5},{2,6},{3,7},{4,0},{5,1},{6,2},{7,3},{8,12},{9,13},{10,... | collective-permute-start | bytes 393224 | tf_op jit(solution)/shard_map/ppermute | solution.py:406
  183.0 6.2 %collective-permute-start.3 = (bf16[1,16,2,1024]{3,1,2,0:T(8,128)(2,1)S(1)}, bf16[1,16,2,1024]{3,1,2,0:T(8,128)(2,1)S(1)}, u32[]{:S(2)}, u32[]{:S(2)}) collective-permute-start(bf16[1,16,2,1024]{3,1,2,0:T(8,128)(2,1)S(1)} %fusion.60), channel_id=1, source_target_pairs={{0,8},{1,9},{2,10},{3,11},{4,12},{5,13},{6,14},{7,15},{8,0},{9,1},... | collective-permute-start | bytes 196616 | tf_op jit(solution)/shard_map/ppermute | solution.py:406
  187.4 5.2 %collective-permute-start.7 = (bf16[1,16,2,1024]{3,1,2,0:T(8,128)(2,1)S(1)}, bf16[1,16,2,1024]{3,1,2,0:T(8,128)(2,1)S(1)}, u32[]{:S(2)}, u32[]{:S(2)}) collective-permute-start(bf16[1,16,2,1024]{3,1,2,0:T(8,128)(2,1)S(1)} %fusion.61), channel_id=1, source_target_pairs={{0,8},{1,9},{2,10},{3,11},{4,12},{5,13},{6,14},{7,15},{8,0},{9,1},... | collective-permute-start | bytes 196616 | tf_op jit(solution)/shard_map/ppermute | solution.py:406
